TPU v7x, 32 devices: a whole 2x2x4 slice. The times are simulated.
32 devices in a mesh: tm: 4 (over x, core), space: 8 (over z, y).
Axes of the slice: x: 2, y: 2, z: 4, core: 2. Of those that a mesh axis runs over, the one named last changes fastest.
Arguments:
- latent_tokens: bfloat16 [16, 8, 64, 64], P('tm', None, 'space'), may hold values from -12 to 12
- conv_in_weight: bfloat16 [3, 3, 3, 16, 384], replicated, may hold values from -0.3125 to 0.3125
- conv_in_bias: float32 [384], replicated, may hold values from -3 to 3
- norm_gain: float32 [384], replicated, may hold values from 0.25 to 1.75
- conv_mid_weight: bfloat16 [3, 3, 3, 384, 384], replicated, may hold values from -0.0625 to 0.0625
- conv_mid_bias: float32 [384], replicated, may hold values from -3 to 3
Outputs:
- decoded: bfloat16 [16, 16, 128, 384], P('tm', 'space')
All inputs are finite; a program needn't handle non-finite values.
Results may differ from a plain program's by a relative error of at most 0.005.
Values may be sent and summed in bfloat16 or wider, within the bound.
No kernel may reach another device: no remote copies, remote signals or barrier semaphores. Data moves between devices by JAX's collectives and lax.ppermute only.
A program may use at most 128 MiB of HBM per device.

v0:
```python
import jax
import jax.numpy as jnp
from jax import lax
from jax.sharding import PartitionSpec as P


def padded_2(cells, sides, width):
    for axis, dim in sides:
        count = lax.axis_size(axis)
        ends = count - 1
        head = lax.slice_in_dim(cells, 0, width, axis=dim)
        tail = lax.slice_in_dim(cells, cells.shape[dim] - width, cells.shape[dim], axis=dim)
        cells = jnp.concatenate(
            [
                lax.ppermute(tail, axis, [(i, (i + 1) % count) for i in range(ends)]),
                cells,
                lax.ppermute(head, axis, [((i + 1) % count, i) for i in range(ends)]),
            ],
            axis=dim,
        )
    return cells


def shifted(value, axis, steps):
    count = lax.axis_size(axis)
    initial, last = (max(0, -steps), min(count, count - steps))
    return lax.ppermute(value, axis, [(source, source + steps) for source in range(initial, last)])


def causal_conv(padded, weight):
    frames = padded.shape[0] - 2
    height = padded.shape[1] - 2
    breadth = padded.shape[2] - 2
    summed = jnp.zeros((frames * height * breadth, weight.shape[-1]), jnp.float32)
    for tap_time in range(3):
        for tap_row in range(3):
            for tap_col in range(3):
                window = padded[
                    tap_time : tap_time + frames,
                    tap_row : tap_row + height,
                    tap_col : tap_col + breadth,
                ]
                summed = summed + jnp.dot(
                    window.reshape(-1, window.shape[-1]),
                    weight[tap_time, tap_row, tap_col],
                    preferred_element_type=jnp.float32,
                )
    return summed.reshape(frames, height, breadth, weight.shape[-1])


def unfold_conv(padded, weight):
    frames = padded.shape[0] - 2
    height = padded.shape[1] - 2
    breadth = padded.shape[2] - 2
    windows = []
    for tap_time in range(3):
        for tap_row in range(3):
            for tap_col in range(3):
                windows.append(
                    padded[
                        tap_time : tap_time + frames,
                        tap_row : tap_row + height,
                        tap_col : tap_col + breadth,
                    ]
                )
    stacked = jnp.concatenate(windows, axis=-1)
    flat_weight = weight.reshape(-1, weight.shape[-1])
    summed = jnp.dot(
        stacked.reshape(-1, stacked.shape[-1]), flat_weight, preferred_element_type=jnp.float32
    )
    return summed.reshape(frames, height, breadth, weight.shape[-1])


def unpatch(tokens):
    frames, height, breadth, _ = tokens.shape
    grid = tokens.reshape(frames, height, breadth, 2, 2, -1).transpose(0, 1, 3, 2, 4, 5)
    return grid.reshape(frames, 2 * height, 2 * breadth, -1)


def activate(feature, norm_gain):
    values = feature.astype(jnp.float32)
    spread = jnp.sqrt(jnp.mean(values * values, axis=-1, keepdims=True) + 1e-06)
    return jax.nn.silu(values / spread * norm_gain).astype(jnp.bfloat16)


def pad_columns(source):
    return jnp.pad(source, ((0, 0), (0, 0), (1, 1), (0, 0)))


def per_device(
    latent_tokens, conv_in_weight, conv_in_bias, norm_gain, conv_mid_weight, conv_mid_bias
):
    tiled = lax.all_to_all(latent_tokens, "space", split_axis=1, concat_axis=2, tiled=True)
    latents = unpatch(tiled)
    rows_ext = padded_2(latents, (("space", 1),), 2)
    cache_rows = shifted(rows_ext, "tm", 1)
    padded = pad_columns(jnp.concatenate([cache_rows, rows_ext], 0))
    feature_ext = (unfold_conv(padded, conv_in_weight) + conv_in_bias).astype(jnp.bfloat16)
    ext_frames = feature_ext.shape[0]
    ext_rows = feature_ext.shape[1]
    frame_keep = jnp.logical_or(jnp.arange(ext_frames) >= 2, lax.axis_index("tm") > 0)
    row_ids = jnp.arange(ext_rows)
    space_at = lax.axis_index("space")
    last_space = lax.axis_size("space") - 1
    top_edge = jnp.logical_and(row_ids == 0, space_at == 0)
    bottom_edge = jnp.logical_and(row_ids == ext_rows - 1, space_at == last_space)
    row_keep = jnp.logical_not(jnp.logical_or(top_edge, bottom_edge))
    keep_mask = jnp.logical_and(frame_keep[:, None], row_keep[None, :]).astype(jnp.bfloat16)[
        :, :, None, None
    ]
    activated = activate(feature_ext, norm_gain) * keep_mask
    padded_act = pad_columns(activated)
    feature = feature_ext[2:, 1:-1]
    mixed_sum = causal_conv(padded_act, conv_mid_weight)
    decoded = (feature.astype(jnp.float32) + mixed_sum + conv_mid_bias).astype(jnp.bfloat16)
    return decoded


def solution(mesh):
    return jax.shard_map(
        per_device,
        mesh=mesh,
        in_specs=(P("tm", None, "space", None), P(), P(), P(), P(), P()),
        out_specs=P("tm", "space", None, None),
        check_vma=False,
    )
```

profile of v0, /device:TPU:1, one launch (start us, length us, event | category | flops | bytes accessed | tf_op | source)
XLA Modules:
  0.0 106.4 jit_solution(564020040830300287)
XLA Ops:
  0.0 0.9 copy.20
  0.9 0.7 reshape.187
  1.6 6.4 %all-to-all-start = ((bf16[8,2,1024]{2,1,0:T(2,128)(2,1)}), bf16[8,2,1024]{2,1,0:T(2,128)(2,1)S(1)}, u32[]{:S(2)}, u32[]{:S(2)}) async-start(bf16[8,2,1024]{2,1,0:T(2,128)(2,1)} %reshape.187), calls=%async_computation | async-start | bytes 65536 | tf_op jit(solution)/shard_map/all_to_all | solution.py:93
  8.0 5.5 %all-to-all-done = bf16[8,2,1024]{2,1,0:T(2,128)(2,1)S(1)} async-done(((bf16[8,2,1024]{2,1,0:T(2,128)(2,1)}), bf16[8,2,1024]{2,1,0:T(2,128)(2,1)S(1)}, u32[]{:S(2)}, u32[]{:S(2)}) %all-to-all-start) | async-done | bytes 32800 | tf_op jit(solution)/shard_map/all_to_all | solution.py:93
  13.6 0.1 reshape.188
  13.7 0.2 reshape.155
  13.8 0.2 copy.14
  14.1 0.1 copy.15
  14.2 1.3 %collective-permute-start.1 = (bf16[4,2,128,16]{2,3,1,0:T(8,128)(2,1)S(1)}, bf16[4,2,128,16]{2,3,1,0:T(8,128)(2,1)S(1)}, u32[]{:S(2)}, u32[]{:S(2)}) collective-permute-start(bf16[4,2,128,16]{2,3,1,0:T(8,128)(2,1)S(1)} %copy.15), channel_id=1, source_target_pairs={{1,0},{2,1},{3,2},{4,3},{5,4},{6,5},{7,6},{9,8},{10,9},{11,10},{12... | collective-permute-start | bytes 98312 | tf_op jit(solution)/shard_map/ppermute | solution.py:17
  15.5 4.0 %collective-permute-start = (bf16[4,2,128,16]{2,3,1,0:T(8,128)(2,1)S(1)}, bf16[4,2,128,16]{2,3,1,0:T(8,128)(2,1)S(1)}, u32[]{:S(2)}, u32[]{:S(2)}) collective-permute-start(bf16[4,2,128,16]{2,3,1,0:T(8,128)(2,1)S(1)} %copy.15), channel_id=1, source_target_pairs={{0,1},{1,2},{2,3},{3,4},{4,5},{5,6},{6,7},{8,9},{9,10},{10,11},{11... | collective-permute-start | bytes 98312 | tf_op jit(solution)/shard_map/ppermute | solution.py:15
  19.5 1.0 collective-permute-done
  20.5 6.2 %collective-permute-start.2 = (bf16[4,6,128,16]{2,3,1,0:T(8,128)(2,1)S(1)}, bf16[4,6,128,16]{2,3,1,0:T(8,128)(2,1)S(1)}, u32[]{:S(2)}, u32[]{:S(2)}) collective-permute-start(bf16[4,6,128,16]{2,3,1,0:T(8,128)(2,1)S(1)} %pad_maximum_fusion), channel_id=1, source_target_pairs={{0,8},{8,16},{16,24},{1,9},{9,17},{17,25},{2,10},{10,18},{18,26},{... | collective-permute-start | bytes 294920 | tf_op jit(solution)/shard_map/ppermute | solution.py:27
  26.8 1.5 %collective-permute-done.2 = bf16[4,6,128,16]{2,3,1,0:T(8,128)(2,1)S(1)} collective-permute-done((bf16[4,6,128,16]{2,3,1,0:T(8,128)(2,1)S(1)}, bf16[4,6,128,16]{2,3,1,0:T(8,128)(2,1)S(1)}, u32[]{:S(2)}, u32[]{:S(2)}) %collective-permute-start.2) | collective-permute-done | bytes 98336 | tf_op jit(solution)/shard_map/ppermute | solution.py:27
  28.5 0.1 fusion.84
  28.6 0.1 fusion.85
  28.8 0.1 fusion.86
  28.9 0.1 fusion.87
  29.0 0.1 fusion.88
  29.2 0.1 fusion.89
  29.3 0.1 fusion.90
  29.4 0.1 fusion.91
  29.6 0.1 fusion.92
  29.7 0.1 fusion.93
  29.8 0.1 fusion.94
  29.9 0.1 fusion.95
  30.1 0.1 fusion.96
  30.2 0.1 fusion.97
  30.3 0.1 fusion.98
  30.5 0.1 fusion.99
  30.6 0.1 fusion.100
  30.7 1.9 %fusion = (f32[6,4,128]{2,1,0:T(4,128)S(1)}, bf16[6,4,128,384]{3,2,1,0:T(8,128)(2,1)S(1)}) fusion(f32[384]{0:T(512)S(1)} %copy-done.5, bf16[6,4,128,432]{2,3,1,0:T(8,128)(2,1)S(1)} %fusion.100, bf16[432,384,1,1]{1,0,3,2:T(8,128)(2,1)S(1)} %bitcast.151), kind=kOutput, calls=%fused_computation.2 | convolution fusion | flops 1025111040 | bytes 5359104 | tf_op jit(solution)/shard_map/dot_general | solution.py:68
  32.7 1.4 %copy-done.2 = bf16[6,4,128,384]{3,2,1,0:T(8,128)(2,1)} copy-done((bf16[6,4,128,384]{3,2,1,0:T(8,128)(2,1)}, bf16[6,4,128,384]{3,2,1,0:T(8,128)(2,1)S(1)}, u32[]{:S(2)}) %copy-start.2) | copy-done | bytes 2359320
  34.1 1.8 %fusion.2 = bf16[6,4,128,384]{3,2,1,0:T(8,128)(2,1)S(1)} fusion(bf16[6,4,128,384]{3,2,1,0:T(8,128)(2,1)S(1)} %get-tuple-element.33, f32[384]{0:T(512)S(1)} %copy-done.3, f32[6,4,128]{2,1,0:T(4,128)S(1)} %add_sqrt_fusion, bf16[6,4]{1,0:T(8,128)(2,1)S(1)} %and_convert_fusion), kind=kLoop, calls=%fused_computation.6 | loop fusion | flops 10616832 | bytes 4732464 | tf_op jit(solution)/shard_map/mul | solution.py:111
  36.0 0.7 pad_slice_fusion.35
  36.7 4.6 %pad_slice_fusion.18 = (bf16[4,2,128,384]{3,2,1,0:T(8,128)(2,1)}, bf16[4,2,128,384]{3,2,1,0:T(8,128)(2,1)S(1)}, bf16[4,2,128,384]{3,2,1,0:T(8,128)(2,1)S(1)}, bf...) fusion(bf16[6,4,128,384]{3,2,1,0:T(8,128)(2,1)S(1)} %fusion.2), kind=kLoop, calls=%fused_computation.140 | loop fusion | bytes 11010048 | tf_op jit(solution)/shard_map/slice | solution.py:38
  41.3 3.5 %fusion.101 = (bf16[4,2,128,384]{3,2,1,0:T(8,128)(2,1)S(1)}, bf16[4,2,128,384]{3,2,1,0:T(8,128)(2,1)S(1)}, bf16[4,2,128,384]{3,2,1,0:T(8,128)(2,1)S(1)}, bf16[4,...) fusion(bf16[6,4,128,384]{3,2,1,0:T(8,128)(2,1)S(1)} %fusion.2), kind=kLoop, calls=%fused_computation.158 | loop fusion | bytes 13369344 | tf_op jit(solution)/shard_map/slice | solution.py:38
  44.9 0.6 fusion.22
  45.5 0.6 fusion.54
  46.1 0.6 fusion.28
  46.8 1.8 %fusion.34 = f32[1024,384]{1,0:T(8,128)} fusion(bf16[1024,384]{1,0:T(8,128)(2,1)S(1)} %bitcast.177, bf16[3,3,3,384,384]{4,3,2,1,0:T(8,128)(2,1)S(1)} %bitcast.153), kind=kOutput, calls=%fused_computation.58 | convolution fusion | flops 301989888 | bytes 2654208 | tf_op jit(solution)/shard_map/dot_general | solution.py:43
  48.6 1.8 %fusion.40 = f32[1024,384]{1,0:T(8,128)} fusion(bf16[1024,384]{1,0:T(8,128)(2,1)S(1)} %bitcast.176, bf16[3,3,3,384,384]{4,3,2,1,0:T(8,128)(2,1)S(1)} %bitcast.153), kind=kOutput, calls=%fused_computation.64 | convolution fusion | flops 301989888 | bytes 2654208 | tf_op jit(solution)/shard_map/dot_general | solution.py:43
  50.4 1.8 %fusion.46 = f32[1024,384]{1,0:T(8,128)} fusion(bf16[1024,384]{1,0:T(8,128)(2,1)S(1)} %bitcast.175, bf16[3,3,3,384,384]{4,3,2,1,0:T(8,128)(2,1)S(1)} %bitcast.153), kind=kOutput, calls=%fused_computation.70 | convolution fusion | flops 301989888 | bytes 2654208 | tf_op jit(solution)/shard_map/dot_general | solution.py:43
  52.2 1.8 %fusion.50 = f32[1024,384]{1,0:T(8,128)} fusion(bf16[1024,384]{1,0:T(8,128)(2,1)S(1)} %bitcast.174, bf16[3,3,3,384,384]{4,3,2,1,0:T(8,128)(2,1)S(1)} %bitcast.153), kind=kOutput, calls=%fused_computation.74 | convolution fusion | flops 301989888 | bytes 2654208 | tf_op jit(solution)/shard_map/dot_general | solution.py:43
  54.0 1.8 %fusion.48 = f32[1024,384]{1,0:T(8,128)} fusion(bf16[1024,384]{1,0:T(8,128)(2,1)S(1)} %bitcast.173, bf16[3,3,3,384,384]{4,3,2,1,0:T(8,128)(2,1)S(1)} %bitcast.153), kind=kOutput, calls=%fused_computation.72 | convolution fusion | flops 301989888 | bytes 2654208 | tf_op jit(solution)/shard_map/dot_general | solution.py:43
  55.8 1.8 %fusion.44 = f32[1024,384]{1,0:T(8,128)} fusion(bf16[1024,384]{1,0:T(8,128)(2,1)S(1)} %bitcast.172, bf16[3,3,3,384,384]{4,3,2,1,0:T(8,128)(2,1)S(1)} %bitcast.153), kind=kOutput, calls=%fused_computation.68 | convolution fusion | flops 301989888 | bytes 2654208 | tf_op jit(solution)/shard_map/dot_general | solution.py:43
  57.5 1.9 %fusion.42 = f32[1024,384]{1,0:T(8,128)} fusion(bf16[1024,384]{1,0:T(8,128)(2,1)S(1)} %bitcast.171, bf16[3,3,3,384,384]{4,3,2,1,0:T(8,128)(2,1)S(1)} %bitcast.153), kind=kOutput, calls=%fused_computation.66 | convolution fusion | flops 301989888 | bytes 2654208 | tf_op jit(solution)/shard_map/dot_general | solution.py:43
  59.4 1.8 %fusion.38 = f32[1024,384]{1,0:T(8,128)} fusion(bf16[1024,384]{1,0:T(8,128)(2,1)S(1)} %bitcast.170, bf16[3,3,3,384,384]{4,3,2,1,0:T(8,128)(2,1)S(1)} %bitcast.153), kind=kOutput, calls=%fused_computation.62 | convolution fusion | flops 301989888 | bytes 2654208 | tf_op jit(solution)/shard_map/dot_general | solution.py:43
  61.2 1.9 %fusion.36 = f32[1024,384]{1,0:T(8,128)} fusion(bf16[1024,384]{1,0:T(8,128)(2,1)S(1)} %bitcast.169, bf16[3,3,3,384,384]{4,3,2,1,0:T(8,128)(2,1)S(1)} %bitcast.153), kind=kOutput, calls=%fused_computation.60 | convolution fusion | flops 301989888 | bytes 2654208 | tf_op jit(solution)/shard_map/dot_general | solution.py:43
  63.1 1.8 %fusion.32 = f32[1024,384]{1,0:T(8,128)} fusion(bf16[1024,384]{1,0:T(8,128)(2,1)S(1)} %bitcast.168, bf16[3,3,3,384,384]{4,3,2,1,0:T(8,128)(2,1)S(1)} %bitcast.153), kind=kOutput, calls=%fused_computation.56 | convolution fusion | flops 301989888 | bytes 2654208 | tf_op jit(solution)/shard_map/dot_general | solution.py:43
  64.9 1.8 %fusion.30 = f32[1024,384]{1,0:T(8,128)} fusion(bf16[1024,384]{1,0:T(8,128)(2,1)S(1)} %bitcast.167, bf16[3,3,3,384,384]{4,3,2,1,0:T(8,128)(2,1)S(1)} %bitcast.153), kind=kOutput, calls=%fused_computation.54 | convolution fusion | flops 301989888 | bytes 2654208 | tf_op jit(solution)/shard_map/dot_general | solution.py:43
  66.7 1.8 %fusion.4 = f32[1024,384]{1,0:T(8,128)} fusion(bf16[1024,384]{1,0:T(8,128)(2,1)S(1)} %bitcast.166, bf16[3,3,3,384,384]{4,3,2,1,0:T(8,128)(2,1)S(1)} %bitcast.153), kind=kOutput, calls=%fused_computation.28 | convolution fusion | flops 301989888 | bytes 2654208 | tf_op jit(solution)/shard_map/dot_general | solution.py:43
  68.4 1.8 %fusion.26 = f32[1024,384]{1,0:T(8,128)} fusion(bf16[1024,384]{1,0:T(8,128)(2,1)S(1)} %bitcast.165, bf16[3,3,3,384,384]{4,3,2,1,0:T(8,128)(2,1)S(1)} %bitcast.153), kind=kOutput, calls=%fused_computation.50 | convolution fusion | flops 301989888 | bytes 2654208 | tf_op jit(solution)/shard_map/dot_general | solution.py:43
  70.2 1.8 %fusion.52 = f32[1024,384]{1,0:T(8,128)} fusion(bf16[1024,384]{1,0:T(8,128)(2,1)S(1)} %bitcast.164, bf16[3,3,3,384,384]{4,3,2,1,0:T(8,128)(2,1)S(1)} %bitcast.153), kind=kOutput, calls=%fused_computation.76 | convolution fusion | flops 301989888 | bytes 2654208 | tf_op jit(solution)/shard_map/dot_general | solution.py:43
  72.0 1.8 %fusion.24 = f32[1024,384]{1,0:T(8,128)} fusion(bf16[1024,384]{1,0:T(8,128)(2,1)S(1)} %bitcast.163, bf16[3,3,3,384,384]{4,3,2,1,0:T(8,128)(2,1)S(1)} %bitcast.153), kind=kOutput, calls=%fused_computation.48 | convolution fusion | flops 301989888 | bytes 2654208 | tf_op jit(solution)/shard_map/dot_general | solution.py:43
  73.8 1.8 %fusion.20 = f32[1024,384]{1,0:T(8,128)} fusion(bf16[1024,384]{1,0:T(8,128)(2,1)S(1)} %bitcast.162, bf16[3,3,3,384,384]{4,3,2,1,0:T(8,128)(2,1)S(1)} %bitcast.153), kind=kOutput, calls=%fused_computation.44 | convolution fusion | flops 301989888 | bytes 2654208 | tf_op jit(solution)/shard_map/dot_general | solution.py:43
  75.6 1.8 %fusion.18 = f32[1024,384]{1,0:T(8,128)} fusion(bf16[1024,384]{1,0:T(8,128)(2,1)S(1)} %bitcast.161, bf16[3,3,3,384,384]{4,3,2,1,0:T(8,128)(2,1)S(1)} %bitcast.153), kind=kOutput, calls=%fused_computation.42 | convolution fusion | flops 301989888 | bytes 2654208 | tf_op jit(solution)/shard_map/dot_general | solution.py:43
  77.4 2.0 %fusion.14 = f32[1024,384]{1,0:T(8,128)} fusion(bf16[1024,384]{1,0:T(8,128)(2,1)S(1)} %bitcast.160, bf16[3,3,3,384,384]{4,3,2,1,0:T(8,128)(2,1)S(1)} %bitcast.153), kind=kOutput, calls=%fused_computation.38 | convolution fusion | flops 301989888 | bytes 2654208 | tf_op jit(solution)/shard_map/dot_general | solution.py:43
  79.4 1.9 %fusion.12 = f32[1024,384]{1,0:T(8,128)} fusion(bf16[1024,384]{1,0:T(8,128)(2,1)S(1)} %bitcast.159, bf16[3,3,3,384,384]{4,3,2,1,0:T(8,128)(2,1)S(1)} %bitcast.153), kind=kOutput, calls=%fused_computation.36 | convolution fusion | flops 301989888 | bytes 2654208 | tf_op jit(solution)/shard_map/dot_general | solution.py:43
  81.3 1.8 %fusion.8 = f32[1024,384]{1,0:T(8,128)} fusion(bf16[1024,384]{1,0:T(8,128)(2,1)S(1)} %bitcast.158, bf16[3,3,3,384,384]{4,3,2,1,0:T(8,128)(2,1)S(1)} %bitcast.153), kind=kOutput, calls=%fused_computation.32 | convolution fusion | flops 301989888 | bytes 2654208 | tf_op jit(solution)/shard_map/dot_general | solution.py:43
  83.1 1.8 %fusion.6 = f32[1024,384]{1,0:T(8,128)} fusion(bf16[1024,384]{1,0:T(8,128)(2,1)S(1)} %bitcast.157, bf16[3,3,3,384,384]{4,3,2,1,0:T(8,128)(2,1)S(1)} %bitcast.153), kind=kOutput, calls=%fused_computation.30 | convolution fusion | flops 301989888 | bytes 2654208 | tf_op jit(solution)/shard_map/dot_general | solution.py:43
  84.9 1.8 %fusion.10 = f32[1024,384]{1,0:T(8,128)} fusion(bf16[1024,384]{1,0:T(8,128)(2,1)S(1)} %bitcast.156, bf16[3,3,3,384,384]{4,3,2,1,0:T(8,128)(2,1)S(1)} %bitcast.153), kind=kOutput, calls=%fused_computation.34 | convolution fusion | flops 301989888 | bytes 2654208 | tf_op jit(solution)/shard_map/dot_general | solution.py:43
  86.6 1.8 %fusion.16 = f32[1024,384]{1,0:T(8,128)} fusion(bf16[1024,384]{1,0:T(8,128)(2,1)S(1)} %bitcast.155, bf16[3,3,3,384,384]{4,3,2,1,0:T(8,128)(2,1)S(1)} %bitcast.153), kind=kOutput, calls=%fused_computation.40 | convolution fusion | flops 301989888 | bytes 2654208 | tf_op jit(solution)/shard_map/dot_general | solution.py:43
  88.4 15.2 %add_add_fusion = f32[1024,384]{1,0:T(8,128)} fusion(f32[1024,384]{1,0:T(8,128)} %fusion.4, f32[1024,384]{1,0:T(8,128)} %fusion.6, f32[1024,384]{1,0:T(8,128)} %fusion.8, f32[1024,384]{1,0:T(8,128)} %fusion.10, f32[1024,384]{1,0:T(8,128)} %fusion.12, f32[1024,384]{1,0:T(8,128)} %fusion.14, f32[1024,384]{1,0:T(8,128)} %fusion.16, f32[1024,384]{1,0:T(8,128)} %fusion.18, ...), kind=kOutput, calls=%fused_computation.8 | convolution fusion | flops 312213504 | bytes 43548672 | tf_op jit(solution)/shard_map/dot_general | solution.py:43
  103.7 2.7 %add_convert_fusion.1 = bf16[4,2,128,384]{3,2,1,0:T(8,128)(2,1)} fusion(f32[4,2,128,384]{3,2,1,0:T(8,128)} %bitcast.154, bf16[6,4,128,384]{3,2,1,0:T(8,128)(2,1)} %copy-done.2, f32[384]{0:T(512)S(1)} %copy-done.4), kind=kLoop, calls=%fused_computation.7 | loop fusion | flops 1572864 | bytes 3147264 | tf_op jit(solution)/shard_map/convert_element_type | solution.py:115
  (34 shorter events, 0.4 us)
Async XLA Ops:
  0.0 30.7 %copy-start = (bf16[3,3,3,16,384]{4,3,2,1,0:T(8,128)(2,1)S(1)}, bf16[3,3,3,16,384]{4,3,2,1,0:T(8,128)(2,1)}, u32[]{:S(2)}) copy-start(bf16[3,3,3,16,384]{4,3,2,1,0:T(8,128)(2,1)} %param.7) | copy-start | bytes 995332
  1.6 11.9 %all-to-all-start = ((bf16[8,2,1024]{2,1,0:T(2,128)(2,1)}), bf16[8,2,1024]{2,1,0:T(2,128)(2,1)S(1)}, u32[]{:S(2)}, u32[]{:S(2)}) async-start(bf16[8,2,1024]{2,1,0:T(2,128)(2,1)} %reshape.187), calls=%async_computation | async-start | bytes 65536 | tf_op jit(solution)/shard_map/all_to_all | solution.py:93
  14.2 5.3 %collective-permute-start.1 = (bf16[4,2,128,16]{2,3,1,0:T(8,128)(2,1)S(1)}, bf16[4,2,128,16]{2,3,1,0:T(8,128)(2,1)S(1)}, u32[]{:S(2)}, u32[]{:S(2)}) collective-permute-start(bf16[4,2,128,16]{2,3,1,0:T(8,128)(2,1)S(1)} %copy.15), channel_id=1, source_target_pairs={{1,0},{2,1},{3,2},{4,3},{5,4},{6,5},{7,6},{9,8},{10,9},{11,10},{12... | collective-permute-start | bytes 98312 | tf_op jit(solution)/shard_map/ppermute | solution.py:17
  15.5 5.0 %collective-permute-start = (bf16[4,2,128,16]{2,3,1,0:T(8,128)(2,1)S(1)}, bf16[4,2,128,16]{2,3,1,0:T(8,128)(2,1)S(1)}, u32[]{:S(2)}, u32[]{:S(2)}) collective-permute-start(bf16[4,2,128,16]{2,3,1,0:T(8,128)(2,1)S(1)} %copy.15), channel_id=1, source_target_pairs={{0,1},{1,2},{2,3},{3,4},{4,5},{5,6},{6,7},{8,9},{9,10},{10,11},{11... | collective-permute-start | bytes 98312 | tf_op jit(solution)/shard_map/ppermute | solution.py:15
  20.5 7.9 %collective-permute-start.2 = (bf16[4,6,128,16]{2,3,1,0:T(8,128)(2,1)S(1)}, bf16[4,6,128,16]{2,3,1,0:T(8,128)(2,1)S(1)}, u32[]{:S(2)}, u32[]{:S(2)}) collective-permute-start(bf16[4,6,128,16]{2,3,1,0:T(8,128)(2,1)S(1)} %pad_maximum_fusion), channel_id=1, source_target_pairs={{0,8},{8,16},{16,24},{1,9},{9,17},{17,25},{2,10},{10,18},{18,26},{... | collective-permute-start | bytes 294920 | tf_op jit(solution)/shard_map/ppermute | solution.py:27
  29.0 1.7 %copy-start.5 = (f32[384]{0:T(512)S(1)}, f32[384]{0:T(512)}, u32[]{:S(2)}) copy-start(f32[384]{0:T(512)} %param.8) | copy-start | bytes 4612
  30.7 3.4 %copy-start.3 = (f32[384]{0:T(512)S(1)}, f32[384]{0:T(512)}, u32[]{:S(2)}) copy-start(f32[384]{0:T(512)} %param.9) | copy-start | bytes 4612
  32.7 1.4 %copy-start.2 = (bf16[6,4,128,384]{3,2,1,0:T(8,128)(2,1)}, bf16[6,4,128,384]{3,2,1,0:T(8,128)(2,1)S(1)}, u32[]{:S(2)}) copy-start(bf16[6,4,128,384]{3,2,1,0:T(8,128)(2,1)S(1)} %get-tuple-element.33) | copy-start | bytes 7077892
  36.7 8.1 %slice-start = ((s8[7962624]{0:T(1024)(128)(4,1)}), s8[4194304]{0:T(1024)(128)(4,1)S(1)}, s32[]{:S(2)}) async-start(s8[7962624]{0:T(1024)(128)(4,1)} %bitcast.152), calls=%async_computation.1 | async-start | bytes 8388608
  41.3 3.5 %slice-start.1 = ((s8[7962624]{0:T(1024)(128)(4,1)}), s8[3768320]{0:T(1024)(128)(4,1)S(1)}, s32[]{:S(2)}) async-start(s8[7962624]{0:T(1024)(128)(4,1)} %bitcast.152), calls=%async_computation.2 | async-start | bytes 7536640
  88.4 15.2 %copy-start.4 = (f32[384]{0:T(512)S(1)}, f32[384]{0:T(512)}, u32[]{:S(2)}) copy-start(f32[384]{0:T(512)} %param.11) | copy-start | bytes 4612
  88.4 17.9 %copy-start.1 = (bf16[3,3,3,16,384]{4,3,2,1,0:T(8,128)(2,1)S(1)}, bf16[3,3,3,16,384]{4,3,2,1,0:T(8,128)(2,1)}, u32[]{:S(2)}) copy-start(bf16[3,3,3,16,384]{4,3,2,1,0:T(8,128)(2,1)} %param.7) | copy-start | bytes 995332
where the time goes:
time: 108 us; the launch traced here: 106 us
  matrix products  60.7 us (56%)
  starting transfers between devices  17.9 us (17%)
  local copies, waits for them, and re-layouts  14.6 us (14%)
  waiting for transfers between devices  8.05 us (7%)
  other arithmetic  4.67 us (4%)
    dot_general x27, matrix products, causal_conv(): jnp.dot(window.reshape(-1, window.shape[-1]), weight[tap_time, tap_row, t...  58.8 us
    slice x3, local copies, waits for them, and re-layouts, causal_conv(): padded[tap_time:tap_time + frames, tap_row:tap_row + height, tap_col:tap_...  8.83 us
    all_to_all x1, starting transfers between devices, per_device(): lax.all_to_all(latent_tokens, 'space', split_axis=1, concat_axis=2, tiled...  6.38 us
    ppermute x1, starting transfers between devices, shifted(): lax.ppermute(value, axis, [(source, source + steps) for source in range(i...  6.24 us
    all_to_all x1, waiting for transfers between devices, per_device(): lax.all_to_all(latent_tokens, 'space', split_axis=1, concat_axis=2, tiled...  5.53 us
    unnamed x45, local copies, waits for them, and re-layouts  5.2 us
    ppermute x1, starting transfers between devices, padded_2(): lax.ppermute(tail, axis, [(i, (i + 1) % count) for i in range(ends)])  3.99 us
    convert_element_type x1, other arithmetic, per_device(): (feature.astype(jnp.float32) + mixed_sum + conv_mid_bias).astype(jnp.bflo...  2.69 us
  transfers between devices with their start and end apart: 4, of which 3 were waited for; matrix products, arithmetic and copies ran while one was open for 0% of the time, Pallas kernels for 0%

commit v1 on v0

v1 whole, which is shorter than its diff:
```python
import functools

import jax
import jax.numpy as jnp
from jax import lax
from jax.experimental import pallas as pl
from jax.experimental.pallas import tpu as pltpu
from jax.sharding import PartitionSpec as P

BF16 = jnp.bfloat16
F32 = jnp.float32
LANES = 128


def dot(left, right):
    return jnp.dot(left, right, preferred_element_type=F32)


def moved_down(value):
    row = lax.broadcasted_iota(jnp.int32, value.shape, 0)
    return jnp.where(row == 0, 0.0, pltpu.roll(value, 1, 0))


def moved_up(value):
    rows = value.shape[0]
    row = lax.broadcasted_iota(jnp.int32, value.shape, 0)
    return jnp.where(row == rows - 1, 0.0, pltpu.roll(value, rows - 1, 0))


def position():
    return lax.axis_index("space")


def chunks_kernel(own_ref, keep_ref, send_ref):
    frames, rows, cols, width = own_ref.shape
    bits = rows.bit_length() - 1
    me = position()
    for relative in range(rows):
        to = [relative >> bit & 1 for bit in range(bits)]
        out_ref = send_ref if to[0] else keep_ref
        tile = me ^ relative
        for near in range(3):
            row = tile + near - 1
            inside = jnp.logical_and(row >= 0, row < rows)
            value = own_ref[:, jnp.clip(row, 0, rows - 1)]
            value = jnp.where(inside, value, jnp.zeros_like(value))
            for pair in range(frames // 2):
                out_ref[(*to[1:], near, pair)] = jnp.concatenate(
                    [value[2 * pair], value[2 * pair + 1]], -1
                )


def token_weight_kernel(conv_in_ref, token_weight_ref):
    ch = conv_in_ref.shape[3]
    mid = conv_in_ref.shape[4]
    token_weight_ref[...] = jnp.zeros_like(token_weight_ref)
    for time in range(3):
        for parity in range(2):
            for near in range(2):
                for b in range(3):
                    for e in range(3):
                        row = near + b
                        col = e + 1 - parity
                        at = (((col // 2) * 2 + row // 2) * 2 + row % 2) * 2 + col % 2
                        token_weight_ref[
                            parity, time, at * ch : (at + 1) * ch, near * mid : (near + 1) * mid
                        ] = conv_in_ref[time, b, e]


def mixed_kernel(time, conv_mid_ref, mixed_ref, taps, arrived):
    mid = conv_mid_ref.shape[-1]
    parts = arrived.shape[0]
    size = mid // parts
    step = 16

    def spread(g0, g1, g2):
        ends = g0 + g2
        return g0, ends + g1, ends - g1, g2

    def one(i, carry):
        at = pl.ds(pl.multiple_of(i * step, step), step)
        cols = [
            spread(*[taps[b, e, at, :].astype(F32) for b in range(3)]) for e in range(3)
        ]
        for u in range(4):
            for v, value in enumerate(spread(*[cols[e][u] for e in range(3)])):
                mixed_ref[u * 4 + v, at, :] = value.astype(BF16)
        return carry

    copies = []
    for part in range(parts):
        at = pl.ds(part * size, size)
        copies.append(
            pltpu.make_async_copy(
                conv_mid_ref.at[time, :, :, at], taps.at[:, :, at], arrived.at[part]
            )
        )
        copies[-1].start()
    for part in range(parts):
        copies[part].wait()
        lax.fori_loop(part * size // step, (part + 1) * size // step, one, 0)


def block_kernel(
    previous_ref,
    own_ref,
    token_weight_ref,
    in_bias_ref,
    gain_ref,
    mixed_0_ref,
    mixed_1_ref,
    mixed_2_ref,
    mid_bias_ref,
    out_ref,
    windows,
    active,
    feature,
    spectrum,
    lines,
):
    tiles, _, pairs, cols, pair = own_ref.shape
    wide = tiles * cols
    frames, rows, _, mid = out_ref.shape
    grown = frames + 2
    width = pair // 2
    me = position()

    with jax.named_scope("windows"):
        for part, ref in enumerate((previous_ref, own_ref)):
            got = [ref[tile ^ me].astype(F32) for tile in range(tiles)]
            for two in range(pairs):
                line = [
                    jnp.concatenate([value[near, two] for value in got], 0) for near in range(3)
                ]
                for half in range(2):
                    above, below = line[half], line[half + 1]
                    for odd in range(2):
                        f = 2 * (part * pairs + two) + odd
                        at = slice(odd * width, (odd + 1) * width)
                        value = jnp.concatenate([above[:, at], below[:, at]], -1)
                        here = value.astype(BF16)
                        windows[0, half, f] = jnp.concatenate(
                            [moved_down(value).astype(BF16), here], -1
                        )
                        windows[1, half, f] = jnp.concatenate(
                            [here, moved_up(value).astype(BF16)], -1
                        )

    in_bias = in_bias_ref[...].reshape(1, mid)
    half_gain = gain_ref[...].reshape(1, mid) * 0.5
    first = (lax.axis_index("tm") > 0).astype(F32)
    top = (me > 0).astype(F32)
    bottom = (me < tiles - 1).astype(F32)
    with jax.named_scope("features"):
        for parity in range(2):
            weight = token_weight_ref[parity].reshape(6 * pair, 2 * mid)
            for half in range(2):
                left = jnp.concatenate(
                    [
                        windows[parity, half, a : a + grown].reshape(grown * wide, 2 * pair)
                        for a in range(3)
                    ],
                    -1,
                )
                summed = dot(left, weight)
                for near in range(2):
                    row = half * 2 + near
                    rounded = (summed[:, near * mid : (near + 1) * mid] + in_bias).astype(BF16)
                    if row in (1, 2):
                        feature[row - 1, parity] = rounded[2 * wide :].reshape(frames, wide, mid)
                    value = rounded.astype(F32)
                    mean = jnp.mean(value * value, axis=-1, keepdims=True)
                    scale = lax.rsqrt(mean + 1e-06)
                    if row == 0:
                        scale = scale * top
                    if row == 3:
                        scale = scale * bottom
                    scale = jnp.concatenate([scale[: 2 * wide] * first, scale[2 * wide :]], 0)
                    h = value * scale * half_gain
                    active[row, parity] = (h + h * jnp.tanh(h)).astype(BF16).reshape(grown, wide, mid)

    with jax.named_scope("spectrum"):

        def one_frame(f, carry):
            cells = []
            for row in range(4):
                even = active[row, 0, f].astype(F32)
                odd = active[row, 1, f].astype(F32)
                cells.append(
                    (moved_down(odd) - odd, even + odd, odd - even, even - moved_up(even))
                )
            for v in range(4):
                r0, r1, r2, r3 = [cells[row][v] for row in range(4)]
                spectrum[v, f] = (r0 - r2).astype(BF16)
                spectrum[4 + v, f] = (r1 + r2).astype(BF16)
                spectrum[8 + v, f] = (r2 - r1).astype(BF16)
                spectrum[12 + v, f] = (r1 - r3).astype(BF16)
            return carry

        lax.fori_loop(0, grown, one_frame, 0)

    def back(m0, m1, m2, m3):
        return m0 + 0.5 * (m1 + m2), 0.5 * (m1 - m2) - m3

    with jax.named_scope("mix"):
        mixed = (mixed_0_ref, mixed_1_ref, mixed_2_ref)
        sums = []
        for u in range(4):
            parts = []
            for v in range(4):
                at = u * 4 + v
                left = jnp.concatenate(
                    [
                        spectrum[at, a : a + frames].reshape(frames * wide, mid)
                        for a in range(3)
                    ],
                    -1,
                )
                right = jnp.concatenate([ref[at] for ref in mixed], 0)
                parts.append(dot(left, right))
            sums.append(back(*parts))
        mid_bias = mid_bias_ref[...].reshape(1, mid)
        for parity in range(2):
            for row, total in enumerate(back(*[sums[u][parity] for u in range(4)])):
                total = (total + mid_bias).reshape(frames, wide, mid)
                total = total + feature[row, parity].astype(F32)
                for f in range(frames):
                    for lane in range(mid // LANES):
                        lines[f, row, lane, pl.ds(parity, wide, stride=2), :] = total[
                            f, :, lane * LANES : (lane + 1) * LANES
                        ]
        for f in range(frames):
            for row in range(rows):
                for lane in range(mid // LANES):
                    out_ref[f, row, :, lane * LANES : (lane + 1) * LANES] = lines[
                        f, row, lane
                    ].astype(BF16)


def limited(mebibytes):
    return pltpu.CompilerParams(vmem_limit_bytes=mebibytes * 2**20)


def after(value, *others):
    return lax.optimization_barrier((value, *others))[0]


def exchanged(keep, send, axis, beside):
    count = lax.axis_size(axis)
    keep, send = keep[None], send[None]
    bit = 1
    while True:
        got = lax.ppermute(send, axis, [(at, at ^ bit) for at in range(count)])
        done = beside(send)
        held = jnp.concatenate([keep, got], 0)
        bit *= 2
        if bit == count:
            return after(held, *done)
        keep, send = held[:, 0], after(held[:, 1], *done)


def shifted(value, axis):
    count = lax.axis_size(axis)
    return lax.ppermute(value, axis, [(at, at + 1) for at in range(count - 1)])


def per_device(
    latent_tokens, conv_in_weight, conv_in_bias, norm_gain, conv_mid_weight, conv_mid_bias
):
    frames, token_rows, cols, width = latent_tokens.shape
    tiles = lax.axis_size("space")
    assert token_rows == tiles and tiles & (tiles - 1) == 0 and frames == 4
    mid = conv_mid_weight.shape[-1]
    wide = tiles * cols
    grown = frames + 2
    line = (3, frames // 2, cols, 2 * width)

    bits = tiles.bit_length() - 1
    half = jax.ShapeDtypeStruct((2,) * (bits - 1) + line, BF16)
    keep, send = pl.pallas_call(chunks_kernel, out_shape=(half, half), compiler_params=limited(2), name="chunks")(
        latent_tokens
    )
    mixed = []

    def beside(value):
        time = len(mixed)
        if time == 3:
            return ()
        mixed.append(
            pl.pallas_call(
                functools.partial(mixed_kernel, time),
                out_shape=pltpu.VMEM((16, mid, mid), BF16),
                in_specs=[pl.BlockSpec(memory_space=pltpu.HBM)],
                scratch_shapes=[
                    pltpu.VMEM((3, 3, mid, mid), BF16),
                    pltpu.SemaphoreType.DMA((4,)),
                ],
                cost_estimate=pl.CostEstimate(
                    flops=0, bytes_accessed=50 * mid * mid, transcendentals=0
                ),
                compiler_params=limited(6),
                name="mixed",
            )(pltpu.with_memory_space_constraint(after(conv_mid_weight, value), pltpu.HBM))
        )
        return mixed[-1:]

    own = exchanged(keep, send, "space", beside)
    while len(mixed) < 3:
        beside(own)
    previous = shifted(own, "tm")
    token_weight = pl.pallas_call(
        token_weight_kernel,
        out_shape=pltpu.VMEM((2, 3, 4 * width, 2 * mid), BF16),
        cost_estimate=pl.CostEstimate(flops=0, bytes_accessed=4 * 2**20, transcendentals=0),
        compiler_params=limited(4),
        name="token_weight",
    )(conv_in_weight)
    held = [pltpu.with_memory_space_constraint(value, pltpu.VMEM) for value in [token_weight, *mixed]]

    return pl.pallas_call(
        block_kernel,
        out_shape=jax.ShapeDtypeStruct((frames, 2, 2 * wide, mid), BF16),
        scratch_shapes=[
            pltpu.VMEM((2, 2, frames + 4, wide, 4 * width), BF16),
            pltpu.VMEM((4, 2, grown, wide, mid), BF16),
            pltpu.VMEM((2, 2, frames, wide, mid), BF16),
            pltpu.VMEM((16, grown, wide, mid), BF16),
            pltpu.VMEM((frames, 2, mid // LANES, 2 * wide, LANES), F32),
        ],
        compiler_params=limited(24),
        name="block",
    )(previous, own, held[0], conv_in_bias, norm_gain, *held[1:], conv_mid_bias)


def solution(mesh):
    return jax.shard_map(
        per_device,
        mesh=mesh,
        in_specs=(P("tm", None, "space", None), P(), P(), P(), P(), P()),
        out_specs=P("tm", "space", None, None),
        check_vma=False,
    )
```

time: 108 us -> 31.9 us (0.30); the launches traced: 106 us -> 31.4 us
  matrix products: 60.7 us -> 0 us
  Pallas kernels: 0 us -> 17.5 us
  local copies, waits for them, and re-layouts: 14.6 us -> 0.86 us
  waiting for transfers between devices: 8.05 us -> 1.37 us
  starting transfers between devices: 17.9 us -> 11.6 us
  other arithmetic: 4.67 us -> 0.04 us
    dot_general x28 -> x0, matrix products: 60.7 us -> none  [the longest x27 58.8 us: causal_conv(): jnp.dot(window.reshape(-1, window.shape[-1]), weight[tap_time, tap_row, t...]
    pallas_call x0 -> x6, Pallas kernels: none -> 17.5 us  [the longest x1 10.9 us: per_device(): pl.pallas_call(block_kernel, out_shape=jax.ShapeDtypeStruct((frames, 2, 2...]
    slice x3 -> x0, local copies, waits for them, and re-layouts: 8.83 us -> none  [causal_conv(): padded[tap_time:tap_time + frames, tap_row:tap_row + height, tap_col:tap_...]
    all_to_all x1 -> x0, starting transfers between devices: 6.38 us -> none  [per_device(): lax.all_to_all(latent_tokens, 'space', split_axis=1, concat_axis=2, tiled...]
    all_to_all x1 -> x0, waiting for transfers between devices: 5.53 us -> none  [per_device(): lax.all_to_all(latent_tokens, 'space', split_axis=1, concat_axis=2, tiled...]
    unnamed x45 -> x10, local copies, waits for them, and re-layouts: 5.2 us -> 0.86 us
    convert_element_type x2 -> x0, other arithmetic: 2.77 us -> none  [the longest x1 2.69 us: per_device(): (feature.astype(jnp.float32) + mixed_sum + conv_mid_bias).astype(jnp.bflo...]
    mul x1 -> x0, other arithmetic: 1.84 us -> none  [per_device(): activated = activate(feature_ext, norm_gain) * keep_mask]
  transfers between devices with their start and end apart: 4 -> 4, of which waited for: 3 -> 1; matrix products, arithmetic and copies ran while one was open for 0% -> 0% of each run, Pallas kernels for 0% -> 21%
where the time goes in v1:
time: 31.9 us; the launch traced here: 31.4 us
  Pallas kernels  17.5 us (55%)
  starting transfers between devices  11.6 us (36%)
  waiting for transfers between devices  1.37 us (4%)
  local copies, waits for them, and re-layouts  0.86 us (3%)
    pallas_call x1, Pallas kernels, per_device(): pl.pallas_call(block_kernel, out_shape=jax.ShapeDtypeStruct((frames, 2, 2...  10.9 us
    pallas_call x3, Pallas kernels, beside(): pl.pallas_call(functools.partial(mixed_kernel, time), out_shape=pltpu.VME...  6.24 us
    ppermute x3, starting transfers between devices, exchanged(): got = lax.ppermute(send, axis, [(at, at ^ bit) for at in range(count)])  5.86 us
    ppermute x1, starting transfers between devices, shifted(): return lax.ppermute(value, axis, [(at, at + 1) for at in range(count - 1)])  5.69 us
    ppermute x1, waiting for transfers between devices, shifted(): return lax.ppermute(value, axis, [(at, at + 1) for at in range(count - 1)])  1.36 us
    unnamed x10, local copies, waits for them, and re-layouts  0.86 us
  transfers between devices with their start and end apart: 4, of which 1 were waited for; matrix products, arithmetic and copies ran while one was open for 0% of the time, Pallas kernels for 21%

profile of v1, /device:TPU:1, one launch (start us, length us, event | category | flops | bytes accessed | tf_op | source)
XLA Modules:
  0.0 31.4 jit_solution(14396404911162435725)
XLA Ops:
  0.0 0.0 copy-start.1
  0.0 0.8 %copy-done.1 = bf16[4,8,8,64]{3,2,1,0:T(8,128)(2,1)S(1)} copy-done((bf16[4,8,8,64]{3,2,1,0:T(8,128)(2,1)S(1)}, bf16[4,8,8,64]{3,2,1,0:T(8,128)(2,1)}, u32[]{:S(2)}) %copy-start.1) | copy-done | bytes 32792
  0.8 0.2 chunks.1
  1.0 2.1 %collective-permute-start = (bf16[1,2,2,3,2,8,128]{6,5,4,3,0,2,1:T(8,128)(2,1)S(1)}, bf16[1,2,2,3,2,8,128]{6,5,4,3,0,2,1:T(8,128)(2,1)S(1)}, u32[]{:S(2)}, u32[]{:S(2)}) collective-permute-start(bf16[1,2,2,3,2,8,128]{6,5,4,3,0,2,1:T(8,128)(2,1)S(1)} %bitcast.11), channel_id=1, source_target_pairs={{0,1},{1,0},{2,3},{3,2},{4,5},{5,4},{6,7},{7,6},{8,9},{9,8},{10,11... | collective-permute-start | bytes 147464 | tf_op jit(solution)/shard_map/ppermute | solution.py:253
  3.1 2.1 %mixed.3.mixed_0_ref = bf16[16,384,384]{2,1,0:T(8,128)(2,1)S(1)} custom-call(bf16[3,3,3,384,384]{4,3,2,1,0:T(8,128)(2,1)} %conv_mid_ref.2), custom_call_target="tpu_custom_call" | custom-call | bytes 7372800 | tf_op jit(solution)/shard_map/mixed/pallas_call | solution.py:290
  5.2 0.0 collective-permute-done
  5.2 1.4 %collective-permute-start.1 = (bf16[2,2,3,2,8,128]{5,4,3,2,0,1:T(8,128)(2,1)S(1)}, bf16[2,2,3,2,8,128]{5,4,3,2,0,1:T(8,128)(2,1)S(1)}, u32[]{:S(2)}, u32[]{:S(2)}) collective-permute-start(bf16[2,2,3,2,8,128]{5,4,3,2,0,1:T(8,128)(2,1)S(1)} %get-tuple-element.16), channel_id=1, source_target_pairs={{0,2},{1,3},{2,0},{3,1},{4,6},{5,7},{6,4},{7,5},{8,10},{9,11},{10,... | collective-permute-start | bytes 147464 | tf_op jit(solution)/shard_map/ppermute | solution.py:253
  6.6 2.1 %mixed.4.mixed_1_ref = bf16[16,384,384]{2,1,0:T(8,128)(2,1)S(1)} custom-call(bf16[3,3,3,384,384]{4,3,2,1,0:T(8,128)(2,1)} %conv_mid_ref.2), custom_call_target="tpu_custom_call" | custom-call | bytes 7372800 | tf_op jit(solution)/shard_map/mixed/pallas_call | solution.py:290
  8.7 0.0 collective-permute-done.1
  8.7 0.0 copy-start
  8.7 0.0 copy-start.2
  8.7 0.0 copy-start.3
  8.8 0.0 copy-start.4
  8.8 2.4 %collective-permute-start.2 = (bf16[4,3,2,8,128]{4,3,2,1,0:T(8,128)(2,1)S(1)}, bf16[4,3,2,8,128]{4,3,2,1,0:T(8,128)(2,1)S(1)}, u32[]{:S(2)}, u32[]{:S(2)}) collective-permute-start(bf16[4,3,2,8,128]{4,3,2,1,0:T(8,128)(2,1)S(1)} %get-tuple-element.18), channel_id=1, source_target_pairs={{0,4},{1,5},{2,6},{3,7},{4,0},{5,1},{6,2},{7,3},{8,12},{9,13},{10,... | collective-permute-start | bytes 147464 | tf_op jit(solution)/shard_map/ppermute | solution.py:253
  11.1 2.1 %mixed.5.mixed_2_ref = bf16[16,384,384]{2,1,0:T(8,128)(2,1)S(1)} custom-call(bf16[3,3,3,384,384]{4,3,2,1,0:T(8,128)(2,1)} %conv_mid_ref.2), custom_call_target="tpu_custom_call" | custom-call | bytes 7372800 | tf_op jit(solution)/shard_map/mixed/pallas_call | solution.py:290
  13.2 0.0 collective-permute-done.2
  13.3 5.7 %collective-permute-start.3 = (bf16[8,3,2,8,128]{4,3,2,1,0:T(8,128)(2,1)S(1)}, bf16[8,3,2,8,128]{4,3,2,1,0:T(8,128)(2,1)S(1)}, u32[]{:S(2)}, u32[]{:S(2)}) collective-permute-start(bf16[8,3,2,8,128]{4,3,2,1,0:T(8,128)(2,1)S(1)} %pad_maximum_fusion.own_ref), channel_id=1, source_target_pairs={{0,8},{8,16},{16,24},{1,9},{9,17},{17,25},{2,10},{10,18},{18,26},{... | collective-permute-start | bytes 294920 | tf_op jit(solution)/shard_map/ppermute | solution.py:264
  19.0 0.0 copy-done
  19.0 0.2 token_weight.1.token_weight_ref
  19.2 1.4 %collective-permute-done.3.previous_ref = bf16[8,3,2,8,128]{4,3,2,1,0:T(8,128)(2,1)S(1)} collective-permute-done((bf16[8,3,2,8,128]{4,3,2,1,0:T(8,128)(2,1)S(1)}, bf16[8,3,2,8,128]{4,3,2,1,0:T(8,128)(2,1)S(1)}, u32[]{:S(2)}, u32[]{:S(2)}) %collective-permute-start.3) | collective-permute-done | bytes 98336 | tf_op jit(solution)/shard_map/ppermute | solution.py:264
  20.6 0.0 copy-done.2
  20.6 0.0 copy-done.3
  20.6 0.0 copy-done.4
  20.6 10.9 %block.1 = bf16[4,2,128,384]{3,2,1,0:T(8,128)(2,1)} custom-call(bf16[8,3,2,8,128]{4,3,2,1,0:T(8,128)(2,1)S(1)} %collective-permute-done.3.previous_ref, bf16[8,3,2,8,128]{4,3,2,1,0:T(8,128)(2,1)S(1)} %pad_maximum_fusion.own_ref, bf16[2,3,256,768]{3,2,1,0:T(8,128)(2,1)S(1)} %token_weight.1.token_weight_ref, f32[384]{0:T(512)S(1)} %copy-done.2, ...), custom_call_target="tpu_custom_call" | custom-call | tf_op jit(solution)/shard_map/block/pallas_call | solution.py:320
  (3 shorter events, 0.0 us)
Async XLA Ops:
  0.0 0.8 %copy-start.1 = (bf16[4,8,8,64]{3,2,1,0:T(8,128)(2,1)S(1)}, bf16[4,8,8,64]{3,2,1,0:T(8,128)(2,1)}, u32[]{:S(2)}) copy-start(bf16[4,8,8,64]{3,2,1,0:T(8,128)(2,1)} %own_ref.1) | copy-start | bytes 98308
  1.0 4.2 %collective-permute-start = (bf16[1,2,2,3,2,8,128]{6,5,4,3,0,2,1:T(8,128)(2,1)S(1)}, bf16[1,2,2,3,2,8,128]{6,5,4,3,0,2,1:T(8,128)(2,1)S(1)}, u32[]{:S(2)}, u32[]{:S(2)}) collective-permute-start(bf16[1,2,2,3,2,8,128]{6,5,4,3,0,2,1:T(8,128)(2,1)S(1)} %bitcast.11), channel_id=1, source_target_pairs={{0,1},{1,0},{2,3},{3,2},{4,5},{5,4},{6,7},{7,6},{8,9},{9,8},{10,11... | collective-permute-start | bytes 147464 | tf_op jit(solution)/shard_map/ppermute | solution.py:253
  5.2 3.5 %collective-permute-start.1 = (bf16[2,2,3,2,8,128]{5,4,3,2,0,1:T(8,128)(2,1)S(1)}, bf16[2,2,3,2,8,128]{5,4,3,2,0,1:T(8,128)(2,1)S(1)}, u32[]{:S(2)}, u32[]{:S(2)}) collective-permute-start(bf16[2,2,3,2,8,128]{5,4,3,2,0,1:T(8,128)(2,1)S(1)} %get-tuple-element.16), channel_id=1, source_target_pairs={{0,2},{1,3},{2,0},{3,1},{4,6},{5,7},{6,4},{7,5},{8,10},{9,11},{10,... | collective-permute-start | bytes 147464 | tf_op jit(solution)/shard_map/ppermute | solution.py:253
  8.7 10.2 %copy-start = (bf16[3,3,3,16,384]{4,3,2,1,0:T(8,128)(2,1)S(1)}, bf16[3,3,3,16,384]{4,3,2,1,0:T(8,128)(2,1)}, u32[]{:S(2)}) copy-start(bf16[3,3,3,16,384]{4,3,2,1,0:T(8,128)(2,1)} %conv_in_ref.1) | copy-start | bytes 995332
  8.7 11.8 %copy-start.2 = (f32[384]{0:T(512)S(1)}, f32[384]{0:T(512)}, u32[]{:S(2)}) copy-start(f32[384]{0:T(512)} %in_bias_ref.1) | copy-start | bytes 4612
  8.7 11.8 %copy-start.3 = (f32[384]{0:T(512)S(1)}, f32[384]{0:T(512)}, u32[]{:S(2)}) copy-start(f32[384]{0:T(512)} %gain_ref.1) | copy-start | bytes 4612
  8.8 11.8 %copy-start.4 = (f32[384]{0:T(512)S(1)}, f32[384]{0:T(512)}, u32[]{:S(2)}) copy-start(f32[384]{0:T(512)} %mid_bias_ref.1) | copy-start | bytes 4612
  8.8 4.5 %collective-permute-start.2 = (bf16[4,3,2,8,128]{4,3,2,1,0:T(8,128)(2,1)S(1)}, bf16[4,3,2,8,128]{4,3,2,1,0:T(8,128)(2,1)S(1)}, u32[]{:S(2)}, u32[]{:S(2)}) collective-permute-start(bf16[4,3,2,8,128]{4,3,2,1,0:T(8,128)(2,1)S(1)} %get-tuple-element.18), channel_id=1, source_target_pairs={{0,4},{1,5},{2,6},{3,7},{4,0},{5,1},{6,2},{7,3},{8,12},{9,13},{10,... | collective-permute-start | bytes 147464 | tf_op jit(solution)/shard_map/ppermute | solution.py:253
  13.3 7.3 %collective-permute-start.3 = (bf16[8,3,2,8,128]{4,3,2,1,0:T(8,128)(2,1)S(1)}, bf16[8,3,2,8,128]{4,3,2,1,0:T(8,128)(2,1)S(1)}, u32[]{:S(2)}, u32[]{:S(2)}) collective-permute-start(bf16[8,3,2,8,128]{4,3,2,1,0:T(8,128)(2,1)S(1)} %pad_maximum_fusion.own_ref), channel_id=1, source_target_pairs={{0,8},{8,16},{16,24},{1,9},{9,17},{17,25},{2,10},{10,18},{18,26},{... | collective-permute-start | bytes 294920 | tf_op jit(solution)/shard_map/ppermute | solution.py:264

commit v2 on v1

--- a/solution.py
+++ b/solution.py
@@ -31,23 +31,33 @@
     return lax.axis_index("space")
 
 
+def place(relative, tiles):
+    bits = tiles.bit_length() - 1
+    return sum((relative >> bit & 1) << (bits - 1 - bit) for bit in range(bits))
+
+
 def chunks_kernel(own_ref, keep_ref, send_ref):
-    frames, rows, cols, width = own_ref.shape
-    bits = rows.bit_length() - 1
-    me = position()
-    for relative in range(rows):
-        to = [relative >> bit & 1 for bit in range(bits)]
-        out_ref = send_ref if to[0] else keep_ref
-        tile = me ^ relative
-        for near in range(3):
-            row = tile + near - 1
+    frames, rows, _, _ = own_ref.shape
+    half = rows // 2
+    mine = position() // half
+    for out_ref, part in ((keep_ref, mine), (send_ref, 1 - mine)):
+        for at in range(half + 2):
+            row = part * half + at - 1
             inside = jnp.logical_and(row >= 0, row < rows)
             value = own_ref[:, jnp.clip(row, 0, rows - 1)]
             value = jnp.where(inside, value, jnp.zeros_like(value))
             for pair in range(frames // 2):
-                out_ref[(*to[1:], near, pair)] = jnp.concatenate(
-                    [value[2 * pair], value[2 * pair + 1]], -1
-                )
+                out_ref[0, at, pair] = jnp.concatenate([value[2 * pair], value[2 * pair + 1]], -1)
+
+
+def halves_kernel(kept_ref, got_ref, keep_ref, send_ref):
+    sources = kept_ref.shape[0]
+    size = keep_ref.shape[1] - 2
+    upper = position() // size % 2
+    for at, ref in enumerate((kept_ref, got_ref)):
+        to = slice(at * sources, (at + 1) * sources)
+        keep_ref[to] = ref[:, pl.ds(upper * size, size + 2)]
+        send_ref[to] = ref[:, pl.ds((1 - upper) * size, size + 2)]
 
 
 def token_weight_kernel(conv_in_ref, token_weight_ref):
@@ -127,7 +137,7 @@
 
     with jax.named_scope("windows"):
         for part, ref in enumerate((previous_ref, own_ref)):
-            got = [ref[tile ^ me].astype(F32) for tile in range(tiles)]
+            got = [ref[place(tile ^ me, tiles)].astype(F32) for tile in range(tiles)]
             for two in range(pairs):
                 line = [
                     jnp.concatenate([value[near, two] for value in got], 0) for near in range(3)
@@ -247,16 +257,18 @@
 
 def exchanged(keep, send, axis, beside):
     count = lax.axis_size(axis)
-    keep, send = keep[None], send[None]
-    bit = 1
+    size = count // 2
     while True:
-        got = lax.ppermute(send, axis, [(at, at ^ bit) for at in range(count)])
+        got = lax.ppermute(send, axis, [(one, one ^ size) for one in range(count)])
         done = beside(send)
-        held = jnp.concatenate([keep, got], 0)
-        bit *= 2
-        if bit == count:
-            return after(held, *done)
-        keep, send = held[:, 0], after(held[:, 1], *done)
+        if size == 1:
+            return after(jnp.concatenate([keep, got], 0), *done)
+        size //= 2
+        half = jax.ShapeDtypeStruct((2 * keep.shape[0], size + 2, *keep.shape[2:]), keep.dtype)
+        keep, send = pl.pallas_call(
+            halves_kernel, out_shape=(half, half), compiler_params=limited(2), name="halves"
+        )(keep, got)
+        send = after(send, *done)
 
 
 def shifted(value, axis):
@@ -273,10 +285,9 @@
     mid = conv_mid_weight.shape[-1]
     wide = tiles * cols
     grown = frames + 2
-    line = (3, frames // 2, cols, 2 * width)
-
-    bits = tiles.bit_length() - 1
-    half = jax.ShapeDtypeStruct((2,) * (bits - 1) + line, BF16)
+    line = (frames // 2, cols, 2 * width)
+
+    half = jax.ShapeDtypeStruct((1, tiles // 2 + 2) + line, BF16)
     keep, send = pl.pallas_call(chunks_kernel, out_shape=(half, half), compiler_params=limited(2), name="chunks")(
         latent_tokens
     )

time: 31.9 us -> 31.3 us (0.981)
  starting transfers between devices: 11.6 us -> 11.2 us
    ppermute x1, starting transfers between devices: 5.69 us -> 5.29 us  [shifted(): return lax.ppermute(value, axis, [(at, at + 1) for at in range(count - 1)])]
where the time goes in v2:
time: 31.3 us; the launch traced here: 31 us
  Pallas kernels  17.5 us (56%)
  starting transfers between devices  11.2 us (36%)
  waiting for transfers between devices  1.37 us (4%)
  local copies, waits for them, and re-layouts  0.86 us (3%)
    pallas_call x1, Pallas kernels, per_device(): pl.pallas_call(block_kernel, out_shape=jax.ShapeDtypeStruct((frames, 2, 2...  10.9 us
    pallas_call x3, Pallas kernels, beside(): pl.pallas_call(functools.partial(mixed_kernel, time), out_shape=pltpu.VME...  6.24 us
    ppermute x3, starting transfers between devices, exchanged(): got = lax.ppermute(send, axis, [(one, one ^ size) for one in range(count)])  5.87 us
    ppermute x1, starting transfers between devices, shifted(): return lax.ppermute(value, axis, [(at, at + 1) for at in range(count - 1)])  5.29 us
    ppermute x1, waiting for transfers between devices, shifted(): return lax.ppermute(value, axis, [(at, at + 1) for at in range(count - 1)])  1.36 us
    unnamed x10, local copies, waits for them, and re-layouts  0.86 us
  transfers between devices with their start and end apart: 4, of which 1 were waited for; matrix products, arithmetic and copies ran while one was open for 0% of the time, Pallas kernels for 21%

profile of v2, /device:TPU:1, one launch (start us, length us, event | category | flops | bytes accessed | tf_op | source)
XLA Modules:
  0.0 31.0 jit_solution(11827570133247895792)
XLA Ops:
  0.0 0.0 copy-start.1
  0.0 0.8 %copy-done.1 = bf16[4,8,8,64]{3,2,1,0:T(8,128)(2,1)S(1)} copy-done((bf16[4,8,8,64]{3,2,1,0:T(8,128)(2,1)S(1)}, bf16[4,8,8,64]{3,2,1,0:T(8,128)(2,1)}, u32[]{:S(2)}) %copy-start.1) | copy-done | bytes 32792
  0.8 0.1 chunks.1
  1.0 3.2 %collective-permute-start = (bf16[1,6,2,8,128]{4,3,2,1,0:T(8,128)(2,1)S(1)}, bf16[1,6,2,8,128]{4,3,2,1,0:T(8,128)(2,1)S(1)}, u32[]{:S(2)}, u32[]{:S(2)}) collective-permute-start(bf16[1,6,2,8,128]{4,3,2,1,0:T(8,128)(2,1)S(1)} %get-tuple-element.18), channel_id=1, source_target_pairs={{0,4},{1,5},{2,6},{3,7},{4,0},{5,1},{6,2},{7,3},{8,12},{9,13},{10,... | collective-permute-start | bytes 73736 | tf_op jit(solution)/shard_map/ppermute | solution.py:262
  4.2 2.1 %mixed.3.mixed_0_ref = bf16[16,384,384]{2,1,0:T(8,128)(2,1)S(1)} custom-call(bf16[3,3,3,384,384]{4,3,2,1,0:T(8,128)(2,1)} %conv_mid_ref.2), custom_call_target="tpu_custom_call" | custom-call | bytes 7372800 | tf_op jit(solution)/shard_map/mixed/pallas_call | solution.py:301
  6.2 0.0 collective-permute-done.got_ref
  6.3 1.4 %collective-permute-start.1 = (bf16[2,4,2,8,128]{4,3,2,1,0:T(8,128)(2,1)S(1)}, bf16[2,4,2,8,128]{4,3,2,1,0:T(8,128)(2,1)S(1)}, u32[]{:S(2)}, u32[]{:S(2)}) collective-permute-start(bf16[2,4,2,8,128]{4,3,2,1,0:T(8,128)(2,1)S(1)} %get-tuple-element.22), channel_id=1, source_target_pairs={{0,2},{1,3},{2,0},{3,1},{4,6},{5,7},{6,4},{7,5},{8,10},{9,11},{10,... | collective-permute-start | bytes 98312 | tf_op jit(solution)/shard_map/ppermute | solution.py:262
  7.6 2.1 %mixed.4.mixed_1_ref = bf16[16,384,384]{2,1,0:T(8,128)(2,1)S(1)} custom-call(bf16[3,3,3,384,384]{4,3,2,1,0:T(8,128)(2,1)} %conv_mid_ref.2), custom_call_target="tpu_custom_call" | custom-call | bytes 7372800 | tf_op jit(solution)/shard_map/mixed/pallas_call | solution.py:301
  9.7 0.0 collective-permute-done.1.got_ref
  9.8 0.0 copy-start
  9.8 0.0 copy-start.2
  9.8 0.0 copy-start.3
  9.8 0.0 copy-start.4
  9.8 1.3 %collective-permute-start.2 = (bf16[4,3,2,8,128]{4,3,2,1,0:T(8,128)(2,1)S(1)}, bf16[4,3,2,8,128]{4,3,2,1,0:T(8,128)(2,1)S(1)}, u32[]{:S(2)}, u32[]{:S(2)}) collective-permute-start(bf16[4,3,2,8,128]{4,3,2,1,0:T(8,128)(2,1)S(1)} %get-tuple-element.26), channel_id=1, source_target_pairs={{0,1},{1,0},{2,3},{3,2},{4,5},{5,4},{6,7},{7,6},{8,9},{9,8},{10,11... | collective-permute-start | bytes 147464 | tf_op jit(solution)/shard_map/ppermute | solution.py:262
  11.1 2.1 %mixed.5.mixed_2_ref = bf16[16,384,384]{2,1,0:T(8,128)(2,1)S(1)} custom-call(bf16[3,3,3,384,384]{4,3,2,1,0:T(8,128)(2,1)} %conv_mid_ref.2), custom_call_target="tpu_custom_call" | custom-call | bytes 7372800 | tf_op jit(solution)/shard_map/mixed/pallas_call | solution.py:301
  13.2 0.0 collective-permute-done.2
  13.2 5.3 %collective-permute-start.3 = (bf16[8,3,2,8,128]{4,3,2,1,0:T(8,128)(2,1)S(1)}, bf16[8,3,2,8,128]{4,3,2,1,0:T(8,128)(2,1)S(1)}, u32[]{:S(2)}, u32[]{:S(2)}) collective-permute-start(bf16[8,3,2,8,128]{4,3,2,1,0:T(8,128)(2,1)S(1)} %pad_maximum_fusion.own_ref), channel_id=1, source_target_pairs={{0,8},{8,16},{16,24},{1,9},{9,17},{17,25},{2,10},{10,18},{18,26},{... | collective-permute-start | bytes 294920 | tf_op jit(solution)/shard_map/ppermute | solution.py:276
  18.5 0.0 copy-done
  18.6 0.2 token_weight.1.token_weight_ref
  18.8 1.4 %collective-permute-done.3.previous_ref = bf16[8,3,2,8,128]{4,3,2,1,0:T(8,128)(2,1)S(1)} collective-permute-done((bf16[8,3,2,8,128]{4,3,2,1,0:T(8,128)(2,1)S(1)}, bf16[8,3,2,8,128]{4,3,2,1,0:T(8,128)(2,1)S(1)}, u32[]{:S(2)}, u32[]{:S(2)}) %collective-permute-start.3) | collective-permute-done | bytes 98336 | tf_op jit(solution)/shard_map/ppermute | solution.py:276
  20.2 0.0 copy-done.2
  20.2 0.0 copy-done.3
  20.2 0.0 copy-done.4
  20.2 10.9 %block.1 = bf16[4,2,128,384]{3,2,1,0:T(8,128)(2,1)} custom-call(bf16[8,3,2,8,128]{4,3,2,1,0:T(8,128)(2,1)S(1)} %collective-permute-done.3.previous_ref, bf16[8,3,2,8,128]{4,3,2,1,0:T(8,128)(2,1)S(1)} %pad_maximum_fusion.own_ref, bf16[2,3,256,768]{3,2,1,0:T(8,128)(2,1)S(1)} %token_weight.1.token_weight_ref, f32[384]{0:T(512)S(1)} %copy-done.2, ...), custom_call_target="tpu_custom_call" | custom-call | tf_op jit(solution)/shard_map/block/pallas_call | solution.py:331
  (3 shorter events, 0.1 us)
Async XLA Ops:
  0.0 0.8 %copy-start.1 = (bf16[4,8,8,64]{3,2,1,0:T(8,128)(2,1)S(1)}, bf16[4,8,8,64]{3,2,1,0:T(8,128)(2,1)}, u32[]{:S(2)}) copy-start(bf16[4,8,8,64]{3,2,1,0:T(8,128)(2,1)} %own_ref.1) | copy-start | bytes 98308
  1.0 5.3 %collective-permute-start = (bf16[1,6,2,8,128]{4,3,2,1,0:T(8,128)(2,1)S(1)}, bf16[1,6,2,8,128]{4,3,2,1,0:T(8,128)(2,1)S(1)}, u32[]{:S(2)}, u32[]{:S(2)}) collective-permute-start(bf16[1,6,2,8,128]{4,3,2,1,0:T(8,128)(2,1)S(1)} %get-tuple-element.18), channel_id=1, source_target_pairs={{0,4},{1,5},{2,6},{3,7},{4,0},{5,1},{6,2},{7,3},{8,12},{9,13},{10,... | collective-permute-start | bytes 73736 | tf_op jit(solution)/shard_map/ppermute | solution.py:262
  6.3 3.5 %collective-permute-start.1 = (bf16[2,4,2,8,128]{4,3,2,1,0:T(8,128)(2,1)S(1)}, bf16[2,4,2,8,128]{4,3,2,1,0:T(8,128)(2,1)S(1)}, u32[]{:S(2)}, u32[]{:S(2)}) collective-permute-start(bf16[2,4,2,8,128]{4,3,2,1,0:T(8,128)(2,1)S(1)} %get-tuple-element.22), channel_id=1, source_target_pairs={{0,2},{1,3},{2,0},{3,1},{4,6},{5,7},{6,4},{7,5},{8,10},{9,11},{10,... | collective-permute-start | bytes 98312 | tf_op jit(solution)/shard_map/ppermute | solution.py:262
  9.8 8.8 %copy-start = (bf16[3,3,3,16,384]{4,3,2,1,0:T(8,128)(2,1)S(1)}, bf16[3,3,3,16,384]{4,3,2,1,0:T(8,128)(2,1)}, u32[]{:S(2)}) copy-start(bf16[3,3,3,16,384]{4,3,2,1,0:T(8,128)(2,1)} %conv_in_ref.1) | copy-start | bytes 995332
  9.8 10.4 %copy-start.2 = (f32[384]{0:T(512)S(1)}, f32[384]{0:T(512)}, u32[]{:S(2)}) copy-start(f32[384]{0:T(512)} %in_bias_ref.1) | copy-start | bytes 4612
  9.8 10.4 %copy-start.3 = (f32[384]{0:T(512)S(1)}, f32[384]{0:T(512)}, u32[]{:S(2)}) copy-start(f32[384]{0:T(512)} %gain_ref.1) | copy-start | bytes 4612
  9.8 10.4 %copy-start.4 = (f32[384]{0:T(512)S(1)}, f32[384]{0:T(512)}, u32[]{:S(2)}) copy-start(f32[384]{0:T(512)} %mid_bias_ref.1) | copy-start | bytes 4612
  9.8 3.4 %collective-permute-start.2 = (bf16[4,3,2,8,128]{4,3,2,1,0:T(8,128)(2,1)S(1)}, bf16[4,3,2,8,128]{4,3,2,1,0:T(8,128)(2,1)S(1)}, u32[]{:S(2)}, u32[]{:S(2)}) collective-permute-start(bf16[4,3,2,8,128]{4,3,2,1,0:T(8,128)(2,1)S(1)} %get-tuple-element.26), channel_id=1, source_target_pairs={{0,1},{1,0},{2,3},{3,2},{4,5},{5,4},{6,7},{7,6},{8,9},{9,8},{10,11... | collective-permute-start | bytes 147464 | tf_op jit(solution)/shard_map/ppermute | solution.py:262
  13.2 6.9 %collective-permute-start.3 = (bf16[8,3,2,8,128]{4,3,2,1,0:T(8,128)(2,1)S(1)}, bf16[8,3,2,8,128]{4,3,2,1,0:T(8,128)(2,1)S(1)}, u32[]{:S(2)}, u32[]{:S(2)}) collective-permute-start(bf16[8,3,2,8,128]{4,3,2,1,0:T(8,128)(2,1)S(1)} %pad_maximum_fusion.own_ref), channel_id=1, source_target_pairs={{0,8},{8,16},{16,24},{1,9},{9,17},{17,25},{2,10},{10,18},{18,26},{... | collective-permute-start | bytes 294920 | tf_op jit(solution)/shard_map/ppermute | solution.py:276

commit v3 on v2

v3 whole, which is shorter than its diff:
```python
import functools

import jax
import jax.numpy as jnp
from jax import lax
from jax.experimental import pallas as pl
from jax.experimental.pallas import tpu as pltpu
from jax.sharding import PartitionSpec as P

BF16 = jnp.bfloat16
F32 = jnp.float32
LANES = 128


def dot(left, right):
    return jnp.dot(left, right, preferred_element_type=F32)


def moved_down(value):
    row = lax.broadcasted_iota(jnp.int32, value.shape, 0)
    return jnp.where(row == 0, 0.0, pltpu.roll(value, 1, 0))


def moved_up(value):
    rows = value.shape[0]
    row = lax.broadcasted_iota(jnp.int32, value.shape, 0)
    return jnp.where(row == rows - 1, 0.0, pltpu.roll(value, rows - 1, 0))


def position():
    return lax.axis_index("space")


def place(relative, tiles):
    bits = tiles.bit_length() - 1
    return sum((relative >> bit & 1) << (bits - 1 - bit) for bit in range(bits))


def chunks_kernel(own_ref, keep_ref, send_ref):
    frames, rows, _, _ = own_ref.shape
    half = rows // 2
    mine = position() // half
    for out_ref, part in ((keep_ref, mine), (send_ref, 1 - mine)):
        for at in range(half + 2):
            row = part * half + at - 1
            inside = jnp.logical_and(row >= 0, row < rows)
            value = own_ref[:, jnp.clip(row, 0, rows - 1)]
            value = jnp.where(inside, value, jnp.zeros_like(value))
            for pair in range(frames // 2):
                out_ref[0, at, pair] = jnp.concatenate([value[2 * pair], value[2 * pair + 1]], -1)


def halves_kernel(kept_ref, got_ref, keep_ref, send_ref):
    sources = kept_ref.shape[0]
    size = keep_ref.shape[1] - 2
    upper = position() // size % 2
    for at, ref in enumerate((kept_ref, got_ref)):
        to = slice(at * sources, (at + 1) * sources)
        keep_ref[to] = ref[:, pl.ds(upper * size, size + 2)]
        send_ref[to] = ref[:, pl.ds((1 - upper) * size, size + 2)]


def token_weight_kernel(conv_in_ref, token_weight_ref):
    ch = conv_in_ref.shape[3]
    mid = conv_in_ref.shape[4]
    for time in range(3):
        for parity in range(2):
            for near in range(2):
                to = slice(near * mid, (near + 1) * mid)
                for row in range(4):
                    for col in range(4):
                        b = row - near
                        e = col - 1 + parity
                        at = (((col // 2) * 2 + row // 2) * 2 + row % 2) * 2 + col % 2
                        inside = 0 <= b < 3 and 0 <= e < 3
                        token_weight_ref[parity, time, at * ch : (at + 1) * ch, to] = (
                            conv_in_ref[time, b, e] if inside else jnp.zeros((ch, mid), BF16)
                        )


def mixed_kernel(time, conv_mid_ref, mixed_ref, taps, arrived):
    mid = conv_mid_ref.shape[-1]
    parts = arrived.shape[0]
    size = mid // parts
    step = 16

    def spread(g0, g1, g2):
        ends = g0 + g2
        return g0, ends + g1, ends - g1, g2

    def one(i, carry):
        at = pl.ds(pl.multiple_of(i * step, step), step)
        cols = [
            spread(*[taps[b, e, at, :].astype(F32) for b in range(3)]) for e in range(3)
        ]
        for u in range(4):
            for v, value in enumerate(spread(*[cols[e][u] for e in range(3)])):
                mixed_ref[u * 4 + v, at, :] = value.astype(BF16)
        return carry

    copies = []
    for part in range(parts):
        at = pl.ds(part * size, size)
        copies.append(
            pltpu.make_async_copy(
                conv_mid_ref.at[time, :, :, at], taps.at[:, :, at], arrived.at[part]
            )
        )
        copies[-1].start()
    for part in range(parts):
        copies[part].wait()
        lax.fori_loop(part * size // step, (part + 1) * size // step, one, 0)


def windows(ref, first, out):
    tiles, _, pairs, cols, pair = ref.shape
    width = pair // 2
    me = position()
    got = [ref[place(tile ^ me, tiles)].astype(F32) for tile in range(tiles)]
    for two in range(pairs):
        line = [jnp.concatenate([value[near, two] for value in got], 0) for near in range(3)]
        for half in range(2):
            above, below = line[half], line[half + 1]
            for odd in range(2):
                f = first + 2 * two + odd
                at = slice(odd * width, (odd + 1) * width)
                value = jnp.concatenate([above[:, at], below[:, at]], -1)
                here = value.astype(BF16)
                out[0, half, f] = jnp.concatenate([moved_down(value).astype(BF16), here], -1)
                out[1, half, f] = jnp.concatenate([here, moved_up(value).astype(BF16)], -1)


def stacked(take, frames):
    return jnp.concatenate(
        [jnp.concatenate([take(f + a) for f in frames], 0) for a in range(3)], -1
    )


def activate(take, frames, blank, tiles, weight_ref, in_bias_ref, gain_ref, active, feature, evens=lambda: None):
    mid = gain_ref.shape[0]
    in_bias = in_bias_ref[...].reshape(1, mid)
    half_gain = gain_ref[...].reshape(1, mid) * 0.5
    me = position()
    started = (lax.axis_index("tm") > 0).astype(F32)
    top = (me > 0).astype(F32)
    bottom = (me < tiles - 1).astype(F32)
    for parity in range(2):
        if parity == 1:
            evens()
        weight = weight_ref[parity].reshape(-1, 2 * mid)
        for half in range(2):
            left = stacked(lambda f: take(parity, half, f), frames)
            wide = left.shape[0] // len(frames)
            summed = dot(left, weight)
            for near in range(2):
                row = half * 2 + near
                rounded = (summed[:, near * mid : (near + 1) * mid] + in_bias).astype(BF16)
                if row in (1, 2):
                    feature[row - 1, parity] = rounded[blank * wide :].reshape(-1, wide, mid)
                value = rounded.astype(F32)
                mean = jnp.mean(value * value, axis=-1, keepdims=True)
                scale = lax.rsqrt(mean + 1e-06)
                if row == 0:
                    scale = scale * top
                if row == 3:
                    scale = scale * bottom
                if blank:
                    scale = jnp.concatenate(
                        [scale[: blank * wide] * started, scale[blank * wide :]], 0
                    )
                h = value * scale * half_gain
                active[row, parity] = (
                    (h + h * jnp.tanh(h)).astype(BF16).reshape(len(frames), wide, mid)
                )


def transform(active, f, u, spectrum, parts=range(4)):
    def over_rows(parity):
        r = [active[row, parity, f].astype(F32) for row in ((0, 2), (1, 2), (2, 1), (1, 3))[u]]
        return r[0] + r[1] if u == 1 else r[0] - r[1]

    even = over_rows(0) if set(parts) - {0} else None
    odd = over_rows(1) if set(parts) - {3} else None
    for v in parts:
        if v == 0:
            value = moved_down(odd) - odd
        elif v == 1:
            value = even + odd
        elif v == 2:
            value = odd - even
        else:
            value = even - moved_up(even)
        spectrum[u * 4 + v, f] = value.astype(BF16)


def front_kernel(
    own_ref, token_weight_ref, in_bias_ref, gain_ref, windows_ref, feature_ref, spectrum_ref, active
):
    windows(own_ref, 0, windows_ref)
    activate(
        lambda parity, half, f: windows_ref[parity, half, f],
        range(windows_ref.shape[2] - 2),
        0,
        own_ref.shape[0],
        token_weight_ref,
        in_bias_ref,
        gain_ref,
        active,
        feature_ref,
    )
    for u in range(4):
        for f in range(active.shape[2]):
            transform(active, f, u, spectrum_ref)


def block_kernel(
    previous_ref,
    windows_ref,
    late_feature_ref,
    late_spectrum_ref,
    token_weight_ref,
    in_bias_ref,
    gain_ref,
    mixed_0_ref,
    mixed_1_ref,
    mixed_2_ref,
    mid_bias_ref,
    out_ref,
    early_windows,
    active,
    feature,
    spectrum,
    lines,
    rounded,
    sent,
):
    tiles = previous_ref.shape[0]
    frames, rows, _, mid = out_ref.shape
    held = early_windows.shape[2]
    early = spectrum.shape[1]
    late = frames - late_feature_ref.shape[2]
    wide = spectrum.shape[2]

    windows(previous_ref, 0, early_windows)
    activate(
        lambda parity, half, f: (
            early_windows[parity, half, f]
            if f < held
            else windows_ref[parity, half, f - held]
        ),
        range(early),
        2,
        tiles,
        token_weight_ref,
        in_bias_ref,
        gain_ref,
        active,
        feature,
        lambda: [transform(active, f, u, spectrum, (3,)) for u in range(4) for f in range(early)],
    )

    def back(m0, m1, m2, m3):
        return m0 + 0.5 * (m1 + m2), 0.5 * (m1 - m2) - m3

    def product(at):
        def take(f):
            return spectrum[at, f] if f < early else late_spectrum_ref[at, f - early]

        right = jnp.concatenate([ref[at] for ref in (mixed_0_ref, mixed_1_ref, mixed_2_ref)], 0)
        return dot(stacked(take, range(frames)), right)

    mid_bias = mid_bias_ref[...].reshape(1, mid)

    def finish(row, totals):
        for parity in range(2):
            total = (totals[parity] + mid_bias).reshape(frames, wide, mid)
            for f in range(frames):
                held_feature = (
                    feature[row, parity, f] if f < late else late_feature_ref[row, parity, f - late]
                )
                value = total[f] + held_feature.astype(F32)
                for lane in range(mid // LANES):
                    lines[f, lane, pl.ds(parity, wide, stride=2), :] = value[
                        :, lane * LANES : (lane + 1) * LANES
                    ]
        for f in range(frames):
            for lane in range(mid // LANES):
                rounded[row, f, :, lane * LANES : (lane + 1) * LANES] = lines[f, lane].astype(BF16)
        copy = pltpu.make_async_copy(rounded.at[row], out_ref.at[:, row], sent.at[row])
        copy.start()
        return copy

    def chores(u):
        return [functools.partial(transform, active, f, u, spectrum, (0, 1, 2)) for f in range(early)]

    last = []
    todo = chores(0) + chores(1)
    for u in range(4):
        last.append(product(u * 4 + 3))
        for chore in todo[2 * u : 2 * u + 2]:
            chore()
    sums = []
    copies = []
    for u in range(4):
        todo = chores(u + 2) if u < 2 else []
        parts = []
        for v in range(3):
            parts.append(product(u * 4 + v))
            for chore in todo[v::3]:
                chore()
        sums.append(back(*parts, last[u]))
        if u == 2:
            totals = [sums[0][p] + 0.5 * (sums[1][p] + sums[2][p]) for p in range(2)]
            copies.append(finish(0, totals))
    totals = [0.5 * (sums[1][p] - sums[2][p]) - sums[3][p] for p in range(2)]
    copies.append(finish(1, totals))
    for copy in copies:
        copy.wait()


def limited(mebibytes):
    return pltpu.CompilerParams(vmem_limit_bytes=mebibytes * 2**20)


def after(value, *others):
    return lax.optimization_barrier((value, *others))[0]


def fast(value):
    return pltpu.with_memory_space_constraint(value, pltpu.VMEM)


def far(value):
    return pltpu.with_memory_space_constraint(value, pltpu.HBM)


def exchanged(keep, send, axis, beside):
    count = lax.axis_size(axis)
    size = count // 2
    while True:
        got = lax.ppermute(send, axis, [(one, one ^ size) for one in range(count)])
        done = beside(send)
        if size == 1:
            return after(jnp.concatenate([keep, got], 0), *done)
        size //= 2
        half = jax.ShapeDtypeStruct((2 * keep.shape[0], size + 2, *keep.shape[2:]), keep.dtype)
        keep, send = pl.pallas_call(
            halves_kernel, out_shape=(half, half), compiler_params=limited(2), name="halves"
        )(keep, got)
        send = after(send, *done)


def shifted(value, axis):
    count = lax.axis_size(axis)
    return lax.ppermute(value, axis, [(at, at + 1) for at in range(count - 1)])


def per_device(
    latent_tokens, conv_in_weight, conv_in_bias, norm_gain, conv_mid_weight, conv_mid_bias
):
    frames, token_rows, cols, width = latent_tokens.shape
    tiles = lax.axis_size("space")
    assert token_rows == tiles and tiles & (tiles - 1) == 0 and frames == 4
    mid = conv_mid_weight.shape[-1]
    wide = tiles * cols
    line = (frames // 2, cols, 2 * width)

    half = jax.ShapeDtypeStruct((1, tiles // 2 + 2) + line, BF16)
    keep, send = pl.pallas_call(chunks_kernel, out_shape=(half, half), compiler_params=limited(2), name="chunks")(
        latent_tokens
    )
    mixed = []

    def beside(value):
        time = len(mixed)
        if time == 3:
            return ()
        weight = far(after(conv_mid_weight, value))
        mixed.append(
            pl.pallas_call(
                functools.partial(mixed_kernel, time),
                out_shape=pltpu.VMEM((16, mid, mid), BF16),
                in_specs=[pl.BlockSpec(memory_space=pltpu.HBM)],
                scratch_shapes=[pltpu.VMEM((3, 3, mid, mid), BF16), pltpu.SemaphoreType.DMA((4,))],
                cost_estimate=pl.CostEstimate(
                    flops=0, bytes_accessed=50 * mid * mid, transcendentals=0
                ),
                compiler_params=limited(6),
                name="mixed",
            )(weight)
        )
        if time < 2:
            return mixed[-1:]
        token_weight.append(
            pl.pallas_call(
                token_weight_kernel,
                out_shape=pltpu.VMEM((2, 3, 4 * width, 2 * mid), BF16),
                cost_estimate=pl.CostEstimate(
                    flops=0, bytes_accessed=4 * 2**20, transcendentals=0
                ),
                compiler_params=limited(4),
                name="token_weight",
            )(conv_in_weight)
        )
        return mixed[-1:] + token_weight

    token_weight = []
    own = exchanged(keep, send, "space", beside)
    while len(mixed) < 3:
        beside(own)
    previous = shifted(own, "tm")

    late = 2
    early = frames + 2 - late
    windows_shape = (2, 2, frames, wide, 4 * width)
    own_windows, late_feature, late_spectrum = pl.pallas_call(
        front_kernel,
        out_shape=(
            pltpu.VMEM(windows_shape, BF16),
            pltpu.VMEM((2, 2, late, wide, mid), BF16),
            pltpu.VMEM((16, late, wide, mid), BF16),
        ),
        scratch_shapes=[pltpu.VMEM((4, 2, late, wide, mid), BF16)],
        cost_estimate=pl.CostEstimate(
            flops=0, bytes_accessed=50 * mid * mid, transcendentals=0
        ),
        compiler_params=limited(8),
        name="front",
    )(own, fast(token_weight[0]), conv_in_bias, norm_gain)

    return pl.pallas_call(
        block_kernel,
        out_shape=jax.ShapeDtypeStruct((frames, 2, 2 * wide, mid), BF16),
        out_specs=pl.BlockSpec(memory_space=pltpu.HBM),
        scratch_shapes=[
            pltpu.VMEM(windows_shape, BF16),
            pltpu.VMEM((4, 2, early, wide, mid), BF16),
            pltpu.VMEM((2, 2, frames - late, wide, mid), BF16),
            pltpu.VMEM((16, early, wide, mid), BF16),
            pltpu.VMEM((frames, mid // LANES, 2 * wide, LANES), F32),
            pltpu.VMEM((2, frames, 2 * wide, mid), BF16),
            pltpu.SemaphoreType.DMA((2,)),
        ],
        compiler_params=limited(24),
        name="block",
    )(
        previous,
        fast(own_windows),
        fast(late_feature),
        fast(late_spectrum),
        fast(token_weight[0]),
        conv_in_bias,
        norm_gain,
        *[fast(value) for value in mixed],
        conv_mid_bias,
    )


def solution(mesh):
    return jax.shard_map(
        per_device,
        mesh=mesh,
        in_specs=(P("tm", None, "space", None), P(), P(), P(), P(), P()),
        out_specs=P("tm", "space", None, None),
        check_vma=False,
    )
```

time: 31.3 us -> 29.6 us (0.946)
  waiting for transfers between devices: 1.37 us -> 0.01 us
    pallas_call x1, Pallas kernels: 10.9 us -> 9.1 us  [per_device(): pl.pallas_call(block_kernel, out_shape=jax.ShapeDtypeStruct((frames, 2, 2...]
    pallas_call x1 -> x2, Pallas kernels: 0.24 us -> 1.88 us  [the longest x1 1.67 us: per_device(): pl.pallas_call(front_kernel, out_shape=(pltpu.VMEM(windows_shape, BF16),...]
    ppermute x1, waiting for transfers between devices: 1.36 us -> 0.01 us  [shifted(): return lax.ppermute(value, axis, [(at, at + 1) for at in range(count - 1)])]
  transfers between devices with their start and end apart: 4 -> 4, of which waited for: 1 -> 0; matrix products, arithmetic and copies ran while one was open for 0% -> 0% of each run, Pallas kernels for 21% -> 28%
where the time goes in v3:
time: 29.6 us; the launch traced here: 29.4 us
  Pallas kernels  17.4 us (59%)
  starting transfers between devices  11 us (37%)
  local copies, waits for them, and re-layouts  0.86 us (3%)
    pallas_call x1, Pallas kernels, per_device(): pl.pallas_call(block_kernel, out_shape=jax.ShapeDtypeStruct((frames, 2, 2...  9.1 us
    pallas_call x3, Pallas kernels, beside(): pl.pallas_call(functools.partial(mixed_kernel, time), out_shape=pltpu.VME...  6.26 us
    ppermute x3, starting transfers between devices, exchanged(): got = lax.ppermute(send, axis, [(one, one ^ size) for one in range(count)])  5.87 us
    ppermute x1, starting transfers between devices, shifted(): return lax.ppermute(value, axis, [(at, at + 1) for at in range(count - 1)])  5.09 us
    pallas_call x1, Pallas kernels, per_device(): pl.pallas_call(front_kernel, out_shape=(pltpu.VMEM(windows_shape, BF16),...  1.67 us
    unnamed x10, local copies, waits for them, and re-layouts  0.86 us
  transfers between devices with their start and end apart: 4, of which 0 were waited for; matrix products, arithmetic and copies ran while one was open for 0% of the time, Pallas kernels for 28%

profile of v3, /device:TPU:1, one launch (start us, length us, event | category | flops | bytes accessed | tf_op | source)
XLA Modules:
  0.0 29.4 jit_solution(3834162370862711602)
XLA Ops:
  0.0 0.0 copy-start.1
  0.0 0.8 %copy-done.1 = bf16[4,8,8,64]{3,2,1,0:T(8,128)(2,1)S(1)} copy-done((bf16[4,8,8,64]{3,2,1,0:T(8,128)(2,1)S(1)}, bf16[4,8,8,64]{3,2,1,0:T(8,128)(2,1)}, u32[]{:S(2)}) %copy-start.1) | copy-done | bytes 32792
  0.8 0.1 chunks.1
  1.0 3.2 %collective-permute-start = (bf16[1,6,2,8,128]{4,3,2,1,0:T(8,128)(2,1)S(1)}, bf16[1,6,2,8,128]{4,3,2,1,0:T(8,128)(2,1)S(1)}, u32[]{:S(2)}, u32[]{:S(2)}) collective-permute-start(bf16[1,6,2,8,128]{4,3,2,1,0:T(8,128)(2,1)S(1)} %get-tuple-element.21), channel_id=1, source_target_pairs={{0,4},{1,5},{2,6},{3,7},{4,0},{5,1},{6,2},{7,3},{8,12},{9,13},{10,... | collective-permute-start | bytes 73736 | tf_op jit(solution)/shard_map/ppermute | solution.py:341
  4.2 2.1 %mixed.3.mixed_0_ref = bf16[16,384,384]{2,1,0:T(8,128)(2,1)S(1)} custom-call(bf16[3,3,3,384,384]{4,3,2,1,0:T(8,128)(2,1)} %conv_mid_ref.2), custom_call_target="tpu_custom_call" | custom-call | bytes 7372800 | tf_op jit(solution)/shard_map/mixed/pallas_call | solution.py:380
  6.2 0.0 collective-permute-done.got_ref
  6.3 0.0 copy-start
  6.3 1.4 %collective-permute-start.1 = (bf16[2,4,2,8,128]{4,3,2,1,0:T(8,128)(2,1)S(1)}, bf16[2,4,2,8,128]{4,3,2,1,0:T(8,128)(2,1)S(1)}, u32[]{:S(2)}, u32[]{:S(2)}) collective-permute-start(bf16[2,4,2,8,128]{4,3,2,1,0:T(8,128)(2,1)S(1)} %get-tuple-element.25), channel_id=1, source_target_pairs={{0,2},{1,3},{2,0},{3,1},{4,6},{5,7},{6,4},{7,5},{8,10},{9,11},{10,... | collective-permute-start | bytes 98312 | tf_op jit(solution)/shard_map/ppermute | solution.py:341
  7.7 2.1 %mixed.4.mixed_1_ref = bf16[16,384,384]{2,1,0:T(8,128)(2,1)S(1)} custom-call(bf16[3,3,3,384,384]{4,3,2,1,0:T(8,128)(2,1)} %conv_mid_ref.2), custom_call_target="tpu_custom_call" | custom-call | bytes 7372800 | tf_op jit(solution)/shard_map/mixed/pallas_call | solution.py:380
  9.7 0.0 collective-permute-done.1.got_ref
  9.8 1.3 %collective-permute-start.2 = (bf16[4,3,2,8,128]{4,3,2,1,0:T(8,128)(2,1)S(1)}, bf16[4,3,2,8,128]{4,3,2,1,0:T(8,128)(2,1)S(1)}, u32[]{:S(2)}, u32[]{:S(2)}) collective-permute-start(bf16[4,3,2,8,128]{4,3,2,1,0:T(8,128)(2,1)S(1)} %get-tuple-element.29), channel_id=1, source_target_pairs={{0,1},{1,0},{2,3},{3,2},{4,5},{5,4},{6,7},{7,6},{8,9},{9,8},{10,11... | collective-permute-start | bytes 147464 | tf_op jit(solution)/shard_map/ppermute | solution.py:341
  11.1 0.0 copy-done
  11.1 0.2 token_weight.1.token_weight_ref
  11.3 0.0 copy-start.2
  11.3 0.0 copy-start.3
  11.3 0.0 copy-start.4
  11.3 2.1 %mixed.5.mixed_2_ref = bf16[16,384,384]{2,1,0:T(8,128)(2,1)S(1)} custom-call(bf16[3,3,3,384,384]{4,3,2,1,0:T(8,128)(2,1)} %conv_mid_ref.2), custom_call_target="tpu_custom_call" | custom-call | bytes 7372800 | tf_op jit(solution)/shard_map/mixed/pallas_call | solution.py:380
  13.4 0.0 collective-permute-done.2
  13.5 5.1 %collective-permute-start.3 = (bf16[8,3,2,8,128]{4,3,2,1,0:T(8,128)(2,1)S(1)}, bf16[8,3,2,8,128]{4,3,2,1,0:T(8,128)(2,1)S(1)}, u32[]{:S(2)}, u32[]{:S(2)}) collective-permute-start(bf16[8,3,2,8,128]{4,3,2,1,0:T(8,128)(2,1)S(1)} %pad_maximum_fusion.own_ref), channel_id=1, source_target_pairs={{0,8},{8,16},{16,24},{1,9},{9,17},{17,25},{2,10},{10,18},{18,26},{... | collective-permute-start | bytes 294920 | tf_op jit(solution)/shard_map/ppermute | solution.py:355
  18.6 0.0 copy-done.2
  18.6 0.0 copy-done.3
  18.6 1.7 %front.1 = (bf16[2,2,4,64,256]{4,3,2,1,0:T(8,128)(2,1)S(1)}, bf16[2,2,2,64,384]{4,3,2,1,0:T(8,128)(2,1)S(1)}, bf16[16,2,64,384]{3,2,1,0:T(8,128)(2,1)S(1)}) custom-call(bf16[8,3,2,8,128]{4,3,2,1,0:T(8,128)(2,1)S(1)} %pad_maximum_fusion.own_ref, bf16[2,3,256,768]{3,2,1,0:T(8,128)(2,1)S(1)} %token_weight.1.token_weight_ref, f32[384]{0:T(512)S(1)} %copy-done.2, ...), custom_call_target="tpu_custom_call" | custom-call | bytes 7372800 | tf_op jit(solution)/shard_map/front/pallas_call | solution.py:416
  20.3 0.0 collective-permute-done.3.previous_ref
  20.3 0.0 copy-done.4
  20.3 9.1 %block.1 = bf16[4,2,128,384]{3,2,1,0:T(8,128)(2,1)} custom-call(bf16[8,3,2,8,128]{4,3,2,1,0:T(8,128)(2,1)S(1)} %collective-permute-done.3.previous_ref, bf16[2,2,4,64,256]{4,3,2,1,0:T(8,128)(2,1)S(1)} %get-tuple-element.32.windows_ref, bf16[2,2,2,64,384]{4,3,2,1,0:T(8,128)(2,1)S(1)} %get-tuple-element.33.late_feature_ref, ...), custom_call_target="tpu_custom_call" | custom-call | tf_op jit(solution)/shard_map/block/pallas_call | solution.py:431
  (3 shorter events, 0.1 us)
Async XLA Ops:
  0.0 0.8 %copy-start.1 = (bf16[4,8,8,64]{3,2,1,0:T(8,128)(2,1)S(1)}, bf16[4,8,8,64]{3,2,1,0:T(8,128)(2,1)}, u32[]{:S(2)}) copy-start(bf16[4,8,8,64]{3,2,1,0:T(8,128)(2,1)} %own_ref.1) | copy-start | bytes 98308
  1.0 5.3 %collective-permute-start = (bf16[1,6,2,8,128]{4,3,2,1,0:T(8,128)(2,1)S(1)}, bf16[1,6,2,8,128]{4,3,2,1,0:T(8,128)(2,1)S(1)}, u32[]{:S(2)}, u32[]{:S(2)}) collective-permute-start(bf16[1,6,2,8,128]{4,3,2,1,0:T(8,128)(2,1)S(1)} %get-tuple-element.21), channel_id=1, source_target_pairs={{0,4},{1,5},{2,6},{3,7},{4,0},{5,1},{6,2},{7,3},{8,12},{9,13},{10,... | collective-permute-start | bytes 73736 | tf_op jit(solution)/shard_map/ppermute | solution.py:341
  6.3 4.8 %copy-start = (bf16[3,3,3,16,384]{4,3,2,1,0:T(8,128)(2,1)S(1)}, bf16[3,3,3,16,384]{4,3,2,1,0:T(8,128)(2,1)}, u32[]{:S(2)}) copy-start(bf16[3,3,3,16,384]{4,3,2,1,0:T(8,128)(2,1)} %conv_in_ref.1) | copy-start | bytes 995332
  6.3 3.5 %collective-permute-start.1 = (bf16[2,4,2,8,128]{4,3,2,1,0:T(8,128)(2,1)S(1)}, bf16[2,4,2,8,128]{4,3,2,1,0:T(8,128)(2,1)S(1)}, u32[]{:S(2)}, u32[]{:S(2)}) collective-permute-start(bf16[2,4,2,8,128]{4,3,2,1,0:T(8,128)(2,1)S(1)} %get-tuple-element.25), channel_id=1, source_target_pairs={{0,2},{1,3},{2,0},{3,1},{4,6},{5,7},{6,4},{7,5},{8,10},{9,11},{10,... | collective-permute-start | bytes 98312 | tf_op jit(solution)/shard_map/ppermute | solution.py:341
  9.8 3.7 %collective-permute-start.2 = (bf16[4,3,2,8,128]{4,3,2,1,0:T(8,128)(2,1)S(1)}, bf16[4,3,2,8,128]{4,3,2,1,0:T(8,128)(2,1)S(1)}, u32[]{:S(2)}, u32[]{:S(2)}) collective-permute-start(bf16[4,3,2,8,128]{4,3,2,1,0:T(8,128)(2,1)S(1)} %get-tuple-element.29), channel_id=1, source_target_pairs={{0,1},{1,0},{2,3},{3,2},{4,5},{5,4},{6,7},{7,6},{8,9},{9,8},{10,11... | collective-permute-start | bytes 147464 | tf_op jit(solution)/shard_map/ppermute | solution.py:341
  11.3 7.3 %copy-start.2 = (f32[384]{0:T(512)S(1)}, f32[384]{0:T(512)}, u32[]{:S(2)}) copy-start(f32[384]{0:T(512)} %in_bias_ref.3) | copy-start | bytes 4612
  11.3 7.3 %copy-start.3 = (f32[384]{0:T(512)S(1)}, f32[384]{0:T(512)}, u32[]{:S(2)}) copy-start(f32[384]{0:T(512)} %gain_ref.3) | copy-start | bytes 4612
  11.3 9.0 %copy-start.4 = (f32[384]{0:T(512)S(1)}, f32[384]{0:T(512)}, u32[]{:S(2)}) copy-start(f32[384]{0:T(512)} %mid_bias_ref.1) | copy-start | bytes 4612
  13.5 6.8 %collective-permute-start.3 = (bf16[8,3,2,8,128]{4,3,2,1,0:T(8,128)(2,1)S(1)}, bf16[8,3,2,8,128]{4,3,2,1,0:T(8,128)(2,1)S(1)}, u32[]{:S(2)}, u32[]{:S(2)}) collective-permute-start(bf16[8,3,2,8,128]{4,3,2,1,0:T(8,128)(2,1)S(1)} %pad_maximum_fusion.own_ref), channel_id=1, source_target_pairs={{0,8},{8,16},{16,24},{1,9},{9,17},{17,25},{2,10},{10,18},{18,26},{... | collective-permute-start | bytes 294920 | tf_op jit(solution)/shard_map/ppermute | solution.py:355

commit v4 on v3

--- a/solution.py
+++ b/solution.py
@@ -10,6 +10,7 @@
 BF16 = jnp.bfloat16
 F32 = jnp.float32
 LANES = 128
+SUBLANES = 8
 
 
 def dot(left, right):
@@ -17,14 +18,20 @@
 
 
 def moved_down(value):
-    row = lax.broadcasted_iota(jnp.int32, value.shape, 0)
-    return jnp.where(row == 0, 0.0, pltpu.roll(value, 1, 0))
+    value = pltpu.roll(value, 1, 0)
+    head = value[:SUBLANES]
+    row = lax.broadcasted_iota(jnp.int32, head.shape, 0)
+    return jnp.concatenate([jnp.where(row == 0, 0.0, head), value[SUBLANES:]], 0)
 
 
 def moved_up(value):
     rows = value.shape[0]
-    row = lax.broadcasted_iota(jnp.int32, value.shape, 0)
-    return jnp.where(row == rows - 1, 0.0, pltpu.roll(value, rows - 1, 0))
+    value = pltpu.roll(value, rows - 1, 0)
+    tail = value[rows - SUBLANES :]
+    row = lax.broadcasted_iota(jnp.int32, tail.shape, 0)
+    return jnp.concatenate(
+        [value[: rows - SUBLANES], jnp.where(row == SUBLANES - 1, 0.0, tail)], 0
+    )
 
 
 def position():
@@ -112,13 +119,15 @@
         lax.fori_loop(part * size // step, (part + 1) * size // step, one, 0)
 
 
-def windows(ref, first, out):
+def windows(ref, first, out, valid=None):
     tiles, _, pairs, cols, pair = ref.shape
     width = pair // 2
     me = position()
     got = [ref[place(tile ^ me, tiles)].astype(F32) for tile in range(tiles)]
     for two in range(pairs):
         line = [jnp.concatenate([value[near, two] for value in got], 0) for near in range(3)]
+        if valid is not None:
+            line = [jnp.where(valid, value, 0.0) for value in line]
         for half in range(2):
             above, below = line[half], line[half + 1]
             for odd in range(2):
@@ -190,7 +199,7 @@
             value = odd - even
         else:
             value = even - moved_up(even)
-        spectrum[u * 4 + v, f] = value.astype(BF16)
+        spectrum[u * 4 + v][f] = value.astype(BF16)
 
 
 def front_kernel(
@@ -208,9 +217,10 @@
         active,
         feature_ref,
     )
+    parts = [spectrum_ref.at[at] for at in range(16)]
     for u in range(4):
         for f in range(active.shape[2]):
-            transform(active, f, u, spectrum_ref)
+            transform(active, f, u, parts)
 
 
 def block_kernel(
@@ -237,11 +247,11 @@
     tiles = previous_ref.shape[0]
     frames, rows, _, mid = out_ref.shape
     held = early_windows.shape[2]
-    early = spectrum.shape[1]
+    early = spectrum[0].shape[0]
     late = frames - late_feature_ref.shape[2]
-    wide = spectrum.shape[2]
-
-    windows(previous_ref, 0, early_windows)
+    wide = spectrum[0].shape[1]
+
+    windows(previous_ref, 0, early_windows, lax.axis_index("tm") > 0)
     activate(
         lambda parity, half, f: (
             early_windows[parity, half, f]
@@ -264,7 +274,7 @@
 
     def product(at):
         def take(f):
-            return spectrum[at, f] if f < early else late_spectrum_ref[at, f - early]
+            return spectrum[at][f] if f < early else late_spectrum_ref[at, f - early]
 
         right = jnp.concatenate([ref[at] for ref in (mixed_0_ref, mixed_1_ref, mixed_2_ref)], 0)
         return dot(stacked(take, range(frames)), right)
@@ -352,7 +362,7 @@
 
 def shifted(value, axis):
     count = lax.axis_size(axis)
-    return lax.ppermute(value, axis, [(at, at + 1) for at in range(count - 1)])
+    return lax.ppermute(value, axis, [(at, (at + 1) % count) for at in range(count)])
 
 
 def per_device(
@@ -436,7 +446,7 @@
             pltpu.VMEM(windows_shape, BF16),
             pltpu.VMEM((4, 2, early, wide, mid), BF16),
             pltpu.VMEM((2, 2, frames - late, wide, mid), BF16),
-            pltpu.VMEM((16, early, wide, mid), BF16),
+            [pltpu.VMEM((early, wide, mid), BF16) for _ in range(16)],
             pltpu.VMEM((frames, mid // LANES, 2 * wide, LANES), F32),
             pltpu.VMEM((2, frames, 2 * wide, mid), BF16),
             pltpu.SemaphoreType.DMA((2,)),

time: 29.6 us -> 28.8 us (0.973)
  the two profiles are of different devices: /device:TPU:1 before, /device:TPU:0 now
where the time goes in v4:
time: 28.8 us; the launch traced here: 28.6 us
  Pallas kernels  17.4 us (60%)
  starting transfers between devices  7.53 us (26%)
  waiting for transfers between devices  2.65 us (9%)
  local copies, waits for them, and re-layouts  0.86 us (3%)
    pallas_call x1, Pallas kernels, per_device(): pl.pallas_call(block_kernel, out_shape=jax.ShapeDtypeStruct((frames, 2, 2...  9.13 us
    ppermute x3, starting transfers between devices, exchanged(): got = lax.ppermute(send, axis, [(one, one ^ size) for one in range(count)])  7.47 us
    pallas_call x3, Pallas kernels, beside(): pl.pallas_call(functools.partial(mixed_kernel, time), out_shape=pltpu.VME...  6.26 us
    ppermute x1, waiting for transfers between devices, shifted(): lax.ppermute(value, axis, [(at, (at + 1) % count) for at in range(count)])  2.32 us
    pallas_call x1, Pallas kernels, per_device(): pl.pallas_call(front_kernel, out_shape=(pltpu.VMEM(windows_shape, BF16),...  1.68 us
    unnamed x10, local copies, waits for them, and re-layouts  0.86 us
  transfers between devices with their start and end apart: 4, of which 3 were waited for; matrix products, arithmetic and copies ran while one was open for 0% of the time, Pallas kernels for 28%

profile of v4, /device:TPU:0, one launch (start us, length us, event | category | flops | bytes accessed | tf_op | source)
XLA Modules:
  0.0 28.6 jit_solution(6784976045190049526)
XLA Ops:
  0.0 0.0 copy-start.1
  0.0 0.8 %copy-done.1 = bf16[4,8,8,64]{3,2,1,0:T(8,128)(2,1)S(1)} copy-done((bf16[4,8,8,64]{3,2,1,0:T(8,128)(2,1)S(1)}, bf16[4,8,8,64]{3,2,1,0:T(8,128)(2,1)}, u32[]{:S(2)}) %copy-start.1) | copy-done | bytes 32792
  0.8 0.1 chunks.1
  1.0 4.1 %collective-permute-start = (bf16[1,6,2,8,128]{4,3,2,1,0:T(8,128)(2,1)S(1)}, bf16[1,6,2,8,128]{4,3,2,1,0:T(8,128)(2,1)S(1)}, u32[]{:S(2)}, u32[]{:S(2)}) collective-permute-start(bf16[1,6,2,8,128]{4,3,2,1,0:T(8,128)(2,1)S(1)} %get-tuple-element.21), channel_id=1, source_target_pairs={{0,4},{1,5},{2,6},{3,7},{4,0},{5,1},{6,2},{7,3},{8,12},{9,13},{10,... | collective-permute-start | bytes 73736 | tf_op jit(solution)/shard_map/ppermute | solution.py:351
  5.1 2.1 %mixed.3.mixed_0_ref = bf16[16,384,384]{2,1,0:T(8,128)(2,1)S(1)} custom-call(bf16[3,3,3,384,384]{4,3,2,1,0:T(8,128)(2,1)} %conv_mid_ref.2), custom_call_target="tpu_custom_call" | custom-call | bytes 7372800 | tf_op jit(solution)/shard_map/mixed/pallas_call | solution.py:390
  7.1 0.0 collective-permute-done.got_ref
  7.2 0.0 copy-start
  7.2 1.6 %collective-permute-start.1 = (bf16[2,4,2,8,128]{4,3,2,1,0:T(8,128)(2,1)S(1)}, bf16[2,4,2,8,128]{4,3,2,1,0:T(8,128)(2,1)S(1)}, u32[]{:S(2)}, u32[]{:S(2)}) collective-permute-start(bf16[2,4,2,8,128]{4,3,2,1,0:T(8,128)(2,1)S(1)} %get-tuple-element.25), channel_id=1, source_target_pairs={{0,2},{1,3},{2,0},{3,1},{4,6},{5,7},{6,4},{7,5},{8,10},{9,11},{10,... | collective-permute-start | bytes 98312 | tf_op jit(solution)/shard_map/ppermute | solution.py:351
  8.8 2.1 %mixed.4.mixed_1_ref = bf16[16,384,384]{2,1,0:T(8,128)(2,1)S(1)} custom-call(bf16[3,3,3,384,384]{4,3,2,1,0:T(8,128)(2,1)} %conv_mid_ref.2), custom_call_target="tpu_custom_call" | custom-call | bytes 7372800 | tf_op jit(solution)/shard_map/mixed/pallas_call | solution.py:390
  10.9 0.2 collective-permute-done.1.got_ref
  11.2 1.7 %collective-permute-start.2 = (bf16[4,3,2,8,128]{4,3,2,1,0:T(8,128)(2,1)S(1)}, bf16[4,3,2,8,128]{4,3,2,1,0:T(8,128)(2,1)S(1)}, u32[]{:S(2)}, u32[]{:S(2)}) collective-permute-start(bf16[4,3,2,8,128]{4,3,2,1,0:T(8,128)(2,1)S(1)} %get-tuple-element.29), channel_id=1, source_target_pairs={{0,1},{1,0},{2,3},{3,2},{4,5},{5,4},{6,7},{7,6},{8,9},{9,8},{10,11... | collective-permute-start | bytes 147464 | tf_op jit(solution)/shard_map/ppermute | solution.py:351
  12.9 0.0 copy-done
  12.9 0.2 token_weight.1.token_weight_ref
  13.1 0.0 copy-start.2
  13.1 0.0 copy-start.3
  13.1 0.0 copy-start.4
  13.2 2.1 %mixed.5.mixed_2_ref = bf16[16,384,384]{2,1,0:T(8,128)(2,1)S(1)} custom-call(bf16[3,3,3,384,384]{4,3,2,1,0:T(8,128)(2,1)} %conv_mid_ref.2), custom_call_target="tpu_custom_call" | custom-call | bytes 7372800 | tf_op jit(solution)/shard_map/mixed/pallas_call | solution.py:390
  15.3 0.1 collective-permute-done.2
  15.4 0.1 collective-permute-start.3
  15.4 0.0 copy-done.2
  15.4 0.0 copy-done.3
  15.4 1.7 %front.1 = (bf16[2,2,4,64,256]{4,3,2,1,0:T(8,128)(2,1)S(1)}, bf16[2,2,2,64,384]{4,3,2,1,0:T(8,128)(2,1)S(1)}, bf16[16,2,64,384]{3,2,1,0:T(8,128)(2,1)S(1)}) custom-call(bf16[8,3,2,8,128]{4,3,2,1,0:T(8,128)(2,1)S(1)} %pad_maximum_fusion.own_ref, bf16[2,3,256,768]{3,2,1,0:T(8,128)(2,1)S(1)} %token_weight.1.token_weight_ref, f32[384]{0:T(512)S(1)} %copy-done.2, ...), custom_call_target="tpu_custom_call" | custom-call | bytes 7372800 | tf_op jit(solution)/shard_map/front/pallas_call | solution.py:426
  17.1 2.3 %collective-permute-done.3.previous_ref = bf16[8,3,2,8,128]{4,3,2,1,0:T(8,128)(2,1)S(1)} collective-permute-done((bf16[8,3,2,8,128]{4,3,2,1,0:T(8,128)(2,1)S(1)}, bf16[8,3,2,8,128]{4,3,2,1,0:T(8,128)(2,1)S(1)}, u32[]{:S(2)}, u32[]{:S(2)}) %collective-permute-start.3) | collective-permute-done | bytes 98336 | tf_op jit(solution)/shard_map/ppermute | solution.py:365
  19.4 0.0 copy-done.4
  19.5 9.1 %block.1 = bf16[4,2,128,384]{3,2,1,0:T(8,128)(2,1)} custom-call(bf16[8,3,2,8,128]{4,3,2,1,0:T(8,128)(2,1)S(1)} %collective-permute-done.3.previous_ref, bf16[2,2,4,64,256]{4,3,2,1,0:T(8,128)(2,1)S(1)} %get-tuple-element.32.windows_ref, bf16[2,2,2,64,384]{4,3,2,1,0:T(8,128)(2,1)S(1)} %get-tuple-element.33.late_feature_ref, ...), custom_call_target="tpu_custom_call" | custom-call | tf_op jit(solution)/shard_map/block/pallas_call | solution.py:441
  (3 shorter events, 0.0 us)
Async XLA Ops:
  0.0 0.8 %copy-start.1 = (bf16[4,8,8,64]{3,2,1,0:T(8,128)(2,1)S(1)}, bf16[4,8,8,64]{3,2,1,0:T(8,128)(2,1)}, u32[]{:S(2)}) copy-start(bf16[4,8,8,64]{3,2,1,0:T(8,128)(2,1)} %own_ref.1) | copy-start | bytes 98308
  1.0 6.2 %collective-permute-start = (bf16[1,6,2,8,128]{4,3,2,1,0:T(8,128)(2,1)S(1)}, bf16[1,6,2,8,128]{4,3,2,1,0:T(8,128)(2,1)S(1)}, u32[]{:S(2)}, u32[]{:S(2)}) collective-permute-start(bf16[1,6,2,8,128]{4,3,2,1,0:T(8,128)(2,1)S(1)} %get-tuple-element.21), channel_id=1, source_target_pairs={{0,4},{1,5},{2,6},{3,7},{4,0},{5,1},{6,2},{7,3},{8,12},{9,13},{10,... | collective-permute-start | bytes 73736 | tf_op jit(solution)/shard_map/ppermute | solution.py:351
  7.2 5.7 %copy-start = (bf16[3,3,3,16,384]{4,3,2,1,0:T(8,128)(2,1)S(1)}, bf16[3,3,3,16,384]{4,3,2,1,0:T(8,128)(2,1)}, u32[]{:S(2)}) copy-start(bf16[3,3,3,16,384]{4,3,2,1,0:T(8,128)(2,1)} %conv_in_ref.1) | copy-start | bytes 995332
  7.2 4.0 %collective-permute-start.1 = (bf16[2,4,2,8,128]{4,3,2,1,0:T(8,128)(2,1)S(1)}, bf16[2,4,2,8,128]{4,3,2,1,0:T(8,128)(2,1)S(1)}, u32[]{:S(2)}, u32[]{:S(2)}) collective-permute-start(bf16[2,4,2,8,128]{4,3,2,1,0:T(8,128)(2,1)S(1)} %get-tuple-element.25), channel_id=1, source_target_pairs={{0,2},{1,3},{2,0},{3,1},{4,6},{5,7},{6,4},{7,5},{8,10},{9,11},{10,... | collective-permute-start | bytes 98312 | tf_op jit(solution)/shard_map/ppermute | solution.py:351
  11.2 4.2 %collective-permute-start.2 = (bf16[4,3,2,8,128]{4,3,2,1,0:T(8,128)(2,1)S(1)}, bf16[4,3,2,8,128]{4,3,2,1,0:T(8,128)(2,1)S(1)}, u32[]{:S(2)}, u32[]{:S(2)}) collective-permute-start(bf16[4,3,2,8,128]{4,3,2,1,0:T(8,128)(2,1)S(1)} %get-tuple-element.29), channel_id=1, source_target_pairs={{0,1},{1,0},{2,3},{3,2},{4,5},{5,4},{6,7},{7,6},{8,9},{9,8},{10,11... | collective-permute-start | bytes 147464 | tf_op jit(solution)/shard_map/ppermute | solution.py:351
  13.1 2.3 %copy-start.2 = (f32[384]{0:T(512)S(1)}, f32[384]{0:T(512)}, u32[]{:S(2)}) copy-start(f32[384]{0:T(512)} %in_bias_ref.3) | copy-start | bytes 4612
  13.1 2.3 %copy-start.3 = (f32[384]{0:T(512)S(1)}, f32[384]{0:T(512)}, u32[]{:S(2)}) copy-start(f32[384]{0:T(512)} %gain_ref.3) | copy-start | bytes 4612
  13.1 6.3 %copy-start.4 = (f32[384]{0:T(512)S(1)}, f32[384]{0:T(512)}, u32[]{:S(2)}) copy-start(f32[384]{0:T(512)} %mid_bias_ref.1) | copy-start | bytes 4612
  15.4 4.1 %collective-permute-start.3 = (bf16[8,3,2,8,128]{4,3,2,1,0:T(8,128)(2,1)S(1)}, bf16[8,3,2,8,128]{4,3,2,1,0:T(8,128)(2,1)S(1)}, u32[]{:S(2)}, u32[]{:S(2)}) collective-permute-start(bf16[8,3,2,8,128]{4,3,2,1,0:T(8,128)(2,1)S(1)} %pad_maximum_fusion.own_ref), channel_id=1, source_target_pairs={{0,8},{8,16},{16,24},{24,0},{1,9},{9,17},{17,25},{25,1},{2,10},{10... | collective-permute-start | bytes 294920 | tf_op jit(solution)/shard_map/ppermute | solution.py:365

commit v5 on v4

--- a/solution.py
+++ b/solution.py
@@ -277,13 +277,14 @@
             return spectrum[at][f] if f < early else late_spectrum_ref[at, f - early]
 
         right = jnp.concatenate([ref[at] for ref in (mixed_0_ref, mixed_1_ref, mixed_2_ref)], 0)
-        return dot(stacked(take, range(frames)), right)
+        left = stacked(take, range(frames))
+        return lax.dot_general(right, left, (((0,), (1,)), ((), ())), preferred_element_type=F32)
 
     mid_bias = mid_bias_ref[...].reshape(1, mid)
 
     def finish(row, totals):
         for parity in range(2):
-            total = (totals[parity] + mid_bias).reshape(frames, wide, mid)
+            total = (totals[parity].T + mid_bias).reshape(frames, wide, mid)
             for f in range(frames):
                 held_feature = (
                     feature[row, parity, f] if f < late else late_feature_ref[row, parity, f - late]

time: 28.8 us -> 27.7 us (0.962)
  Pallas kernels: 17.4 us -> 16.3 us
    pallas_call x1, Pallas kernels: 9.13 us -> 8.02 us  [per_device(): pl.pallas_call(block_kernel, out_shape=jax.ShapeDtypeStruct((frames, 2, 2...]
  transfers between devices with their start and end apart: 4 -> 4, of which waited for: 3 -> 3; matrix products, arithmetic and copies ran while one was open for 0% -> 0% of each run, Pallas kernels for 28% -> 30%
where the time goes in v5:
time: 27.7 us; the launch traced here: 27.5 us
  Pallas kernels  16.3 us (59%)
  starting transfers between devices  7.53 us (27%)
  waiting for transfers between devices  2.65 us (10%)
  local copies, waits for them, and re-layouts  0.86 us (3%)
    pallas_call x1, Pallas kernels, per_device(): pl.pallas_call(block_kernel, out_shape=jax.ShapeDtypeStruct((frames, 2, 2...  8.02 us
    ppermute x3, starting transfers between devices, exchanged(): got = lax.ppermute(send, axis, [(one, one ^ size) for one in range(count)])  7.47 us
    pallas_call x3, Pallas kernels, beside(): pl.pallas_call(functools.partial(mixed_kernel, time), out_shape=pltpu.VME...  6.26 us
    ppermute x1, waiting for transfers between devices, shifted(): lax.ppermute(value, axis, [(at, (at + 1) % count) for at in range(count)])  2.32 us
    pallas_call x1, Pallas kernels, per_device(): pl.pallas_call(front_kernel, out_shape=(pltpu.VMEM(windows_shape, BF16),...  1.68 us
    unnamed x10, local copies, waits for them, and re-layouts  0.86 us
  transfers between devices with their start and end apart: 4, of which 3 were waited for; matrix products, arithmetic and copies ran while one was open for 0% of the time, Pallas kernels for 30%

profile of v5, /device:TPU:0, one launch (start us, length us, event | category | flops | bytes accessed | tf_op | source)
XLA Modules:
  0.0 27.5 jit_solution(14633898587750694822)
XLA Ops:
  0.0 0.0 copy-start.1
  0.0 0.8 %copy-done.1 = bf16[4,8,8,64]{3,2,1,0:T(8,128)(2,1)S(1)} copy-done((bf16[4,8,8,64]{3,2,1,0:T(8,128)(2,1)S(1)}, bf16[4,8,8,64]{3,2,1,0:T(8,128)(2,1)}, u32[]{:S(2)}) %copy-start.1) | copy-done | bytes 32792
  0.8 0.1 chunks.1
  1.0 4.1 %collective-permute-start = (bf16[1,6,2,8,128]{4,3,2,1,0:T(8,128)(2,1)S(1)}, bf16[1,6,2,8,128]{4,3,2,1,0:T(8,128)(2,1)S(1)}, u32[]{:S(2)}, u32[]{:S(2)}) collective-permute-start(bf16[1,6,2,8,128]{4,3,2,1,0:T(8,128)(2,1)S(1)} %get-tuple-element.21), channel_id=1, source_target_pairs={{0,4},{1,5},{2,6},{3,7},{4,0},{5,1},{6,2},{7,3},{8,12},{9,13},{10,... | collective-permute-start | bytes 73736 | tf_op jit(solution)/shard_map/ppermute | solution.py:352
  5.1 2.1 %mixed.3.mixed_0_ref = bf16[16,384,384]{2,1,0:T(8,128)(2,1)S(1)} custom-call(bf16[3,3,3,384,384]{4,3,2,1,0:T(8,128)(2,1)} %conv_mid_ref.2), custom_call_target="tpu_custom_call" | custom-call | bytes 7372800 | tf_op jit(solution)/shard_map/mixed/pallas_call | solution.py:391
  7.1 0.0 collective-permute-done.got_ref
  7.2 0.0 copy-start
  7.2 1.6 %collective-permute-start.1 = (bf16[2,4,2,8,128]{4,3,2,1,0:T(8,128)(2,1)S(1)}, bf16[2,4,2,8,128]{4,3,2,1,0:T(8,128)(2,1)S(1)}, u32[]{:S(2)}, u32[]{:S(2)}) collective-permute-start(bf16[2,4,2,8,128]{4,3,2,1,0:T(8,128)(2,1)S(1)} %get-tuple-element.25), channel_id=1, source_target_pairs={{0,2},{1,3},{2,0},{3,1},{4,6},{5,7},{6,4},{7,5},{8,10},{9,11},{10,... | collective-permute-start | bytes 98312 | tf_op jit(solution)/shard_map/ppermute | solution.py:352
  8.8 2.1 %mixed.4.mixed_1_ref = bf16[16,384,384]{2,1,0:T(8,128)(2,1)S(1)} custom-call(bf16[3,3,3,384,384]{4,3,2,1,0:T(8,128)(2,1)} %conv_mid_ref.2), custom_call_target="tpu_custom_call" | custom-call | bytes 7372800 | tf_op jit(solution)/shard_map/mixed/pallas_call | solution.py:391
  10.9 0.2 collective-permute-done.1.got_ref
  11.2 1.7 %collective-permute-start.2 = (bf16[4,3,2,8,128]{4,3,2,1,0:T(8,128)(2,1)S(1)}, bf16[4,3,2,8,128]{4,3,2,1,0:T(8,128)(2,1)S(1)}, u32[]{:S(2)}, u32[]{:S(2)}) collective-permute-start(bf16[4,3,2,8,128]{4,3,2,1,0:T(8,128)(2,1)S(1)} %get-tuple-element.29), channel_id=1, source_target_pairs={{0,1},{1,0},{2,3},{3,2},{4,5},{5,4},{6,7},{7,6},{8,9},{9,8},{10,11... | collective-permute-start | bytes 147464 | tf_op jit(solution)/shard_map/ppermute | solution.py:352
  12.9 0.0 copy-done
  12.9 0.2 token_weight.1.token_weight_ref
  13.1 0.0 copy-start.2
  13.1 0.0 copy-start.3
  13.1 0.0 copy-start.4
  13.2 2.1 %mixed.5.mixed_2_ref = bf16[16,384,384]{2,1,0:T(8,128)(2,1)S(1)} custom-call(bf16[3,3,3,384,384]{4,3,2,1,0:T(8,128)(2,1)} %conv_mid_ref.2), custom_call_target="tpu_custom_call" | custom-call | bytes 7372800 | tf_op jit(solution)/shard_map/mixed/pallas_call | solution.py:391
  15.3 0.1 collective-permute-done.2
  15.4 0.1 collective-permute-start.3
  15.4 0.0 copy-done.2
  15.4 0.0 copy-done.3
  15.4 1.7 %front.1 = (bf16[2,2,4,64,256]{4,3,2,1,0:T(8,128)(2,1)S(1)}, bf16[2,2,2,64,384]{4,3,2,1,0:T(8,128)(2,1)S(1)}, bf16[16,2,64,384]{3,2,1,0:T(8,128)(2,1)S(1)}) custom-call(bf16[8,3,2,8,128]{4,3,2,1,0:T(8,128)(2,1)S(1)} %pad_maximum_fusion.own_ref, bf16[2,3,256,768]{3,2,1,0:T(8,128)(2,1)S(1)} %token_weight.1.token_weight_ref, f32[384]{0:T(512)S(1)} %copy-done.2, ...), custom_call_target="tpu_custom_call" | custom-call | bytes 7372800 | tf_op jit(solution)/shard_map/front/pallas_call | solution.py:427
  17.1 2.3 %collective-permute-done.3.previous_ref = bf16[8,3,2,8,128]{4,3,2,1,0:T(8,128)(2,1)S(1)} collective-permute-done((bf16[8,3,2,8,128]{4,3,2,1,0:T(8,128)(2,1)S(1)}, bf16[8,3,2,8,128]{4,3,2,1,0:T(8,128)(2,1)S(1)}, u32[]{:S(2)}, u32[]{:S(2)}) %collective-permute-start.3) | collective-permute-done | bytes 98336 | tf_op jit(solution)/shard_map/ppermute | solution.py:366
  19.4 0.0 copy-done.4
  19.5 8.0 %block.1 = bf16[4,2,128,384]{3,2,1,0:T(8,128)(2,1)} custom-call(bf16[8,3,2,8,128]{4,3,2,1,0:T(8,128)(2,1)S(1)} %collective-permute-done.3.previous_ref, bf16[2,2,4,64,256]{4,3,2,1,0:T(8,128)(2,1)S(1)} %get-tuple-element.32.windows_ref, bf16[2,2,2,64,384]{4,3,2,1,0:T(8,128)(2,1)S(1)} %get-tuple-element.33.late_feature_ref, ...), custom_call_target="tpu_custom_call" | custom-call | tf_op jit(solution)/shard_map/block/pallas_call | solution.py:442
  (3 shorter events, 0.0 us)
Async XLA Ops:
  0.0 0.8 %copy-start.1 = (bf16[4,8,8,64]{3,2,1,0:T(8,128)(2,1)S(1)}, bf16[4,8,8,64]{3,2,1,0:T(8,128)(2,1)}, u32[]{:S(2)}) copy-start(bf16[4,8,8,64]{3,2,1,0:T(8,128)(2,1)} %own_ref.1) | copy-start | bytes 98308
  1.0 6.2 %collective-permute-start = (bf16[1,6,2,8,128]{4,3,2,1,0:T(8,128)(2,1)S(1)}, bf16[1,6,2,8,128]{4,3,2,1,0:T(8,128)(2,1)S(1)}, u32[]{:S(2)}, u32[]{:S(2)}) collective-permute-start(bf16[1,6,2,8,128]{4,3,2,1,0:T(8,128)(2,1)S(1)} %get-tuple-element.21), channel_id=1, source_target_pairs={{0,4},{1,5},{2,6},{3,7},{4,0},{5,1},{6,2},{7,3},{8,12},{9,13},{10,... | collective-permute-start | bytes 73736 | tf_op jit(solution)/shard_map/ppermute | solution.py:352
  7.2 5.7 %copy-start = (bf16[3,3,3,16,384]{4,3,2,1,0:T(8,128)(2,1)S(1)}, bf16[3,3,3,16,384]{4,3,2,1,0:T(8,128)(2,1)}, u32[]{:S(2)}) copy-start(bf16[3,3,3,16,384]{4,3,2,1,0:T(8,128)(2,1)} %conv_in_ref.1) | copy-start | bytes 995332
  7.2 4.0 %collective-permute-start.1 = (bf16[2,4,2,8,128]{4,3,2,1,0:T(8,128)(2,1)S(1)}, bf16[2,4,2,8,128]{4,3,2,1,0:T(8,128)(2,1)S(1)}, u32[]{:S(2)}, u32[]{:S(2)}) collective-permute-start(bf16[2,4,2,8,128]{4,3,2,1,0:T(8,128)(2,1)S(1)} %get-tuple-element.25), channel_id=1, source_target_pairs={{0,2},{1,3},{2,0},{3,1},{4,6},{5,7},{6,4},{7,5},{8,10},{9,11},{10,... | collective-permute-start | bytes 98312 | tf_op jit(solution)/shard_map/ppermute | solution.py:352
  11.2 4.2 %collective-permute-start.2 = (bf16[4,3,2,8,128]{4,3,2,1,0:T(8,128)(2,1)S(1)}, bf16[4,3,2,8,128]{4,3,2,1,0:T(8,128)(2,1)S(1)}, u32[]{:S(2)}, u32[]{:S(2)}) collective-permute-start(bf16[4,3,2,8,128]{4,3,2,1,0:T(8,128)(2,1)S(1)} %get-tuple-element.29), channel_id=1, source_target_pairs={{0,1},{1,0},{2,3},{3,2},{4,5},{5,4},{6,7},{7,6},{8,9},{9,8},{10,11... | collective-permute-start | bytes 147464 | tf_op jit(solution)/shard_map/ppermute | solution.py:352
  13.1 2.3 %copy-start.2 = (f32[384]{0:T(512)S(1)}, f32[384]{0:T(512)}, u32[]{:S(2)}) copy-start(f32[384]{0:T(512)} %in_bias_ref.3) | copy-start | bytes 4612
  13.1 2.3 %copy-start.3 = (f32[384]{0:T(512)S(1)}, f32[384]{0:T(512)}, u32[]{:S(2)}) copy-start(f32[384]{0:T(512)} %gain_ref.3) | copy-start | bytes 4612
  13.1 6.3 %copy-start.4 = (f32[384]{0:T(512)S(1)}, f32[384]{0:T(512)}, u32[]{:S(2)}) copy-start(f32[384]{0:T(512)} %mid_bias_ref.1) | copy-start | bytes 4612
  15.4 4.1 %collective-permute-start.3 = (bf16[8,3,2,8,128]{4,3,2,1,0:T(8,128)(2,1)S(1)}, bf16[8,3,2,8,128]{4,3,2,1,0:T(8,128)(2,1)S(1)}, u32[]{:S(2)}, u32[]{:S(2)}) collective-permute-start(bf16[8,3,2,8,128]{4,3,2,1,0:T(8,128)(2,1)S(1)} %pad_maximum_fusion.own_ref), channel_id=1, source_target_pairs={{0,8},{8,16},{16,24},{24,0},{1,9},{9,17},{17,25},{25,1},{2,10},{10... | collective-permute-start | bytes 294920 | tf_op jit(solution)/shard_map/ppermute | solution.py:366

commit v6 on v4

--- a/solution.py
+++ b/solution.py
@@ -119,15 +119,13 @@
         lax.fori_loop(part * size // step, (part + 1) * size // step, one, 0)
 
 
-def windows(ref, first, out, valid=None):
+def windows(ref, first, out):
     tiles, _, pairs, cols, pair = ref.shape
     width = pair // 2
     me = position()
     got = [ref[place(tile ^ me, tiles)].astype(F32) for tile in range(tiles)]
     for two in range(pairs):
         line = [jnp.concatenate([value[near, two] for value in got], 0) for near in range(3)]
-        if valid is not None:
-            line = [jnp.where(valid, value, 0.0) for value in line]
         for half in range(2):
             above, below = line[half], line[half + 1]
             for odd in range(2):
@@ -145,12 +143,11 @@
     )
 
 
-def activate(take, frames, blank, tiles, weight_ref, in_bias_ref, gain_ref, active, feature, evens=lambda: None):
+def activate(take, frames, skip, tiles, weight_ref, in_bias_ref, gain_ref, active, feature, evens=lambda: None):
     mid = gain_ref.shape[0]
     in_bias = in_bias_ref[...].reshape(1, mid)
     half_gain = gain_ref[...].reshape(1, mid) * 0.5
     me = position()
-    started = (lax.axis_index("tm") > 0).astype(F32)
     top = (me > 0).astype(F32)
     bottom = (me < tiles - 1).astype(F32)
     for parity in range(2):
@@ -165,7 +162,7 @@
                 row = half * 2 + near
                 rounded = (summed[:, near * mid : (near + 1) * mid] + in_bias).astype(BF16)
                 if row in (1, 2):
-                    feature[row - 1, parity] = rounded[blank * wide :].reshape(-1, wide, mid)
+                    feature[row - 1, parity] = rounded[skip * wide :].reshape(-1, wide, mid)
                 value = rounded.astype(F32)
                 mean = jnp.mean(value * value, axis=-1, keepdims=True)
                 scale = lax.rsqrt(mean + 1e-06)
@@ -173,12 +170,8 @@
                     scale = scale * top
                 if row == 3:
                     scale = scale * bottom
-                if blank:
-                    scale = jnp.concatenate(
-                        [scale[: blank * wide] * started, scale[blank * wide :]], 0
-                    )
                 h = value * scale * half_gain
-                active[row, parity] = (
+                active[row, parity, frames.start : frames.stop] = (
                     (h + h * jnp.tanh(h)).astype(BF16).reshape(len(frames), wide, mid)
                 )
 
@@ -251,81 +244,95 @@
     late = frames - late_feature_ref.shape[2]
     wide = spectrum[0].shape[1]
 
-    windows(previous_ref, 0, early_windows, lax.axis_index("tm") > 0)
-    activate(
-        lambda parity, half, f: (
-            early_windows[parity, half, f]
-            if f < held
-            else windows_ref[parity, half, f - held]
-        ),
-        range(early),
-        2,
-        tiles,
-        token_weight_ref,
-        in_bias_ref,
-        gain_ref,
-        active,
-        feature,
-        lambda: [transform(active, f, u, spectrum, (3,)) for u in range(4) for f in range(early)],
-    )
-
-    def back(m0, m1, m2, m3):
-        return m0 + 0.5 * (m1 + m2), 0.5 * (m1 - m2) - m3
-
-    def product(at):
-        def take(f):
-            return spectrum[at][f] if f < early else late_spectrum_ref[at, f - early]
-
-        right = jnp.concatenate([ref[at] for ref in (mixed_0_ref, mixed_1_ref, mixed_2_ref)], 0)
-        return dot(stacked(take, range(frames)), right)
-
-    mid_bias = mid_bias_ref[...].reshape(1, mid)
-
-    def finish(row, totals):
-        for parity in range(2):
-            total = (totals[parity] + mid_bias).reshape(frames, wide, mid)
+    def run(start):
+        if start == 0:
+            windows(previous_ref, 0, early_windows)
+
+        def window(parity, half, f):
+            if f >= held:
+                return windows_ref[parity, half, f - held]
+            if start:
+                return jnp.zeros(early_windows.shape[3:], BF16)
+            return early_windows[parity, half, f]
+
+        activate(
+            window,
+            range(start, early),
+            2 - start,
+            tiles,
+            token_weight_ref,
+            in_bias_ref,
+            gain_ref,
+            active,
+            feature,
+            lambda: [
+                transform(active, f, u, spectrum, (3,)) for u in range(4) for f in range(start, early)
+            ],
+        )
+
+        def back(m0, m1, m2, m3):
+            return m0 + 0.5 * (m1 + m2), 0.5 * (m1 - m2) - m3
+
+        def product(at):
+            def take(f):
+                if f < start:
+                    return jnp.zeros((wide, mid), BF16)
+                return spectrum[at][f] if f < early else late_spectrum_ref[at, f - early]
+
+            right = jnp.concatenate([ref[at] for ref in (mixed_0_ref, mixed_1_ref, mixed_2_ref)], 0)
+            left = stacked(take, range(frames))
+            return lax.dot_general(right, left, (((0,), (1,)), ((), ())), preferred_element_type=F32)
+
+        mid_bias = mid_bias_ref[...].reshape(1, mid)
+
+        def finish(row, totals):
+            for parity in range(2):
+                total = (totals[parity].T + mid_bias).reshape(frames, wide, mid)
+                for f in range(frames):
+                    held_feature = (
+                        feature[row, parity, f] if f < late else late_feature_ref[row, parity, f - late]
+                    )
+                    value = total[f] + held_feature.astype(F32)
+                    for lane in range(mid // LANES):
+                        lines[f, lane, pl.ds(parity, wide, stride=2), :] = value[
+                            :, lane * LANES : (lane + 1) * LANES
+                        ]
             for f in range(frames):
-                held_feature = (
-                    feature[row, parity, f] if f < late else late_feature_ref[row, parity, f - late]
-                )
-                value = total[f] + held_feature.astype(F32)
                 for lane in range(mid // LANES):
-                    lines[f, lane, pl.ds(parity, wide, stride=2), :] = value[
-                        :, lane * LANES : (lane + 1) * LANES
-                    ]
-        for f in range(frames):
-            for lane in range(mid // LANES):
-                rounded[row, f, :, lane * LANES : (lane + 1) * LANES] = lines[f, lane].astype(BF16)
-        copy = pltpu.make_async_copy(rounded.at[row], out_ref.at[:, row], sent.at[row])
-        copy.start()
-        return copy
-
-    def chores(u):
-        return [functools.partial(transform, active, f, u, spectrum, (0, 1, 2)) for f in range(early)]
-
-    last = []
-    todo = chores(0) + chores(1)
-    for u in range(4):
-        last.append(product(u * 4 + 3))
-        for chore in todo[2 * u : 2 * u + 2]:
-            chore()
-    sums = []
-    copies = []
-    for u in range(4):
-        todo = chores(u + 2) if u < 2 else []
-        parts = []
-        for v in range(3):
-            parts.append(product(u * 4 + v))
-            for chore in todo[v::3]:
+                    rounded[row, f, :, lane * LANES : (lane + 1) * LANES] = lines[f, lane].astype(BF16)
+            copy = pltpu.make_async_copy(rounded.at[row], out_ref.at[:, row], sent.at[row])
+            copy.start()
+            return copy
+
+        def chores(u):
+            return [functools.partial(transform, active, f, u, spectrum, (0, 1, 2)) for f in range(start, early)]
+
+        last = []
+        todo = chores(0) + chores(1)
+        for u in range(4):
+            last.append(product(u * 4 + 3))
+            for chore in todo[u::4]:
                 chore()
-        sums.append(back(*parts, last[u]))
-        if u == 2:
-            totals = [sums[0][p] + 0.5 * (sums[1][p] + sums[2][p]) for p in range(2)]
-            copies.append(finish(0, totals))
-    totals = [0.5 * (sums[1][p] - sums[2][p]) - sums[3][p] for p in range(2)]
-    copies.append(finish(1, totals))
-    for copy in copies:
-        copy.wait()
+        sums = []
+        copies = []
+        for u in range(4):
+            todo = chores(u + 2) if u < 2 else []
+            parts = []
+            for v in range(3):
+                parts.append(product(u * 4 + v))
+                for chore in todo[v::3]:
+                    chore()
+            sums.append(back(*parts, last[u]))
+            if u == 2:
+                totals = [sums[0][p] + 0.5 * (sums[1][p] + sums[2][p]) for p in range(2)]
+                copies.append(finish(0, totals))
+        totals = [0.5 * (sums[1][p] - sums[2][p]) - sums[3][p] for p in range(2)]
+        copies.append(finish(1, totals))
+        for copy in copies:
+            copy.wait()
+
+    pl.when(lax.axis_index("tm") > 0)(lambda: run(0))
+    pl.when(lax.axis_index("tm") == 0)(lambda: run(2))
 
 
 def limited(mebibytes):

time: 28.8 us -> 26.6 us (0.924)
  the two profiles are of different devices: /device:TPU:0 before, /device:TPU:1 now
where the time goes in v6:
time: 26.6 us; the launch traced here: 26.4 us
  Pallas kernels  16.1 us (61%)
  starting transfers between devices  9.1 us (34%)
  local copies, waits for them, and re-layouts  0.86 us (3%)
  between operations  0.3 us (1%)
    pallas_call x1, Pallas kernels, per_device(): pl.pallas_call(block_kernel, out_shape=jax.ShapeDtypeStruct((frames, 2, 2...  7.81 us
    pallas_call x3, Pallas kernels, beside(): pl.pallas_call(functools.partial(mixed_kernel, time), out_shape=pltpu.VME...  6.26 us
    ppermute x3, starting transfers between devices, exchanged(): got = lax.ppermute(send, axis, [(one, one ^ size) for one in range(count)])  5.87 us
    ppermute x1, starting transfers between devices, shifted(): lax.ppermute(value, axis, [(at, (at + 1) % count) for at in range(count)])  3.23 us
    pallas_call x1, Pallas kernels, per_device(): pl.pallas_call(front_kernel, out_shape=(pltpu.VMEM(windows_shape, BF16),...  1.68 us
    unnamed x10, local copies, waits for them, and re-layouts  0.86 us
  transfers between devices with their start and end apart: 4, of which 0 were waited for; matrix products, arithmetic and copies ran while one was open for 0% of the time, Pallas kernels for 31%

profile of v6, /device:TPU:1, one launch (start us, length us, event | category | flops | bytes accessed | tf_op | source)
XLA Modules:
  0.0 26.4 jit_solution(3303095605505189995)
XLA Ops:
  0.0 0.0 copy-start.1
  0.0 0.8 %copy-done.1 = bf16[4,8,8,64]{3,2,1,0:T(8,128)(2,1)S(1)} copy-done((bf16[4,8,8,64]{3,2,1,0:T(8,128)(2,1)S(1)}, bf16[4,8,8,64]{3,2,1,0:T(8,128)(2,1)}, u32[]{:S(2)}) %copy-start.1) | copy-done | bytes 32792
  0.8 0.1 chunks.1
  1.0 3.2 %collective-permute-start = (bf16[1,6,2,8,128]{4,3,2,1,0:T(8,128)(2,1)S(1)}, bf16[1,6,2,8,128]{4,3,2,1,0:T(8,128)(2,1)S(1)}, u32[]{:S(2)}, u32[]{:S(2)}) collective-permute-start(bf16[1,6,2,8,128]{4,3,2,1,0:T(8,128)(2,1)S(1)} %get-tuple-element.21), channel_id=1, source_target_pairs={{0,4},{1,5},{2,6},{3,7},{4,0},{5,1},{6,2},{7,3},{8,12},{9,13},{10,... | collective-permute-start | bytes 73736 | tf_op jit(solution)/shard_map/ppermute | solution.py:358
  4.2 2.1 %mixed.3.mixed_0_ref = bf16[16,384,384]{2,1,0:T(8,128)(2,1)S(1)} custom-call(bf16[3,3,3,384,384]{4,3,2,1,0:T(8,128)(2,1)} %conv_mid_ref.2), custom_call_target="tpu_custom_call" | custom-call | bytes 7372800 | tf_op jit(solution)/shard_map/mixed/pallas_call | solution.py:397
  6.2 0.0 collective-permute-done.got_ref
  6.3 0.0 copy-start
  6.3 1.4 %collective-permute-start.1 = (bf16[2,4,2,8,128]{4,3,2,1,0:T(8,128)(2,1)S(1)}, bf16[2,4,2,8,128]{4,3,2,1,0:T(8,128)(2,1)S(1)}, u32[]{:S(2)}, u32[]{:S(2)}) collective-permute-start(bf16[2,4,2,8,128]{4,3,2,1,0:T(8,128)(2,1)S(1)} %get-tuple-element.25), channel_id=1, source_target_pairs={{0,2},{1,3},{2,0},{3,1},{4,6},{5,7},{6,4},{7,5},{8,10},{9,11},{10,... | collective-permute-start | bytes 98312 | tf_op jit(solution)/shard_map/ppermute | solution.py:358
  7.7 2.1 %mixed.4.mixed_1_ref = bf16[16,384,384]{2,1,0:T(8,128)(2,1)S(1)} custom-call(bf16[3,3,3,384,384]{4,3,2,1,0:T(8,128)(2,1)} %conv_mid_ref.2), custom_call_target="tpu_custom_call" | custom-call | bytes 7372800 | tf_op jit(solution)/shard_map/mixed/pallas_call | solution.py:397
  9.7 0.0 collective-permute-done.1.got_ref
  9.8 1.3 %collective-permute-start.2 = (bf16[4,3,2,8,128]{4,3,2,1,0:T(8,128)(2,1)S(1)}, bf16[4,3,2,8,128]{4,3,2,1,0:T(8,128)(2,1)S(1)}, u32[]{:S(2)}, u32[]{:S(2)}) collective-permute-start(bf16[4,3,2,8,128]{4,3,2,1,0:T(8,128)(2,1)S(1)} %get-tuple-element.29), channel_id=1, source_target_pairs={{0,1},{1,0},{2,3},{3,2},{4,5},{5,4},{6,7},{7,6},{8,9},{9,8},{10,11... | collective-permute-start | bytes 147464 | tf_op jit(solution)/shard_map/ppermute | solution.py:358
  11.1 0.0 copy-done
  11.1 0.2 token_weight.1.token_weight_ref
  11.3 0.0 copy-start.2
  11.3 0.0 copy-start.3
  11.3 0.0 copy-start.4
  11.3 2.1 %mixed.5.mixed_2_ref = bf16[16,384,384]{2,1,0:T(8,128)(2,1)S(1)} custom-call(bf16[3,3,3,384,384]{4,3,2,1,0:T(8,128)(2,1)} %conv_mid_ref.2), custom_call_target="tpu_custom_call" | custom-call | bytes 7372800 | tf_op jit(solution)/shard_map/mixed/pallas_call | solution.py:397
  13.4 0.0 collective-permute-done.2
  13.5 3.2 %collective-permute-start.3 = (bf16[8,3,2,8,128]{4,3,2,1,0:T(8,128)(2,1)S(1)}, bf16[8,3,2,8,128]{4,3,2,1,0:T(8,128)(2,1)S(1)}, u32[]{:S(2)}, u32[]{:S(2)}) collective-permute-start(bf16[8,3,2,8,128]{4,3,2,1,0:T(8,128)(2,1)S(1)} %pad_maximum_fusion.own_ref), channel_id=1, source_target_pairs={{0,8},{8,16},{16,24},{24,0},{1,9},{9,17},{17,25},{25,1},{2,10},{10... | collective-permute-start | bytes 294920 | tf_op jit(solution)/shard_map/ppermute | solution.py:372
  16.7 0.0 copy-done.2
  16.7 0.0 copy-done.3
  16.7 1.7 %front.1 = (bf16[2,2,4,64,256]{4,3,2,1,0:T(8,128)(2,1)S(1)}, bf16[2,2,2,64,384]{4,3,2,1,0:T(8,128)(2,1)S(1)}, bf16[16,2,64,384]{3,2,1,0:T(8,128)(2,1)S(1)}) custom-call(bf16[8,3,2,8,128]{4,3,2,1,0:T(8,128)(2,1)S(1)} %pad_maximum_fusion.own_ref, bf16[2,3,256,768]{3,2,1,0:T(8,128)(2,1)S(1)} %token_weight.1.token_weight_ref, f32[384]{0:T(512)S(1)} %copy-done.2, ...), custom_call_target="tpu_custom_call" | custom-call | bytes 7372800 | tf_op jit(solution)/shard_map/front/pallas_call | solution.py:433
  18.4 0.0 collective-permute-done.3.previous_ref
  18.4 0.0 copy-done.4
  18.4 7.8 %block.1 = bf16[4,2,128,384]{3,2,1,0:T(8,128)(2,1)} custom-call(bf16[8,3,2,8,128]{4,3,2,1,0:T(8,128)(2,1)S(1)} %collective-permute-done.3.previous_ref, bf16[2,2,4,64,256]{4,3,2,1,0:T(8,128)(2,1)S(1)} %get-tuple-element.32.windows_ref, bf16[2,2,2,64,384]{4,3,2,1,0:T(8,128)(2,1)S(1)} %get-tuple-element.33.late_feature_ref, ...), custom_call_target="tpu_custom_call" | custom-call | tf_op jit(solution)/shard_map/block/pallas_call | solution.py:448
  (3 shorter events, 0.1 us)
Async XLA Ops:
  0.0 0.8 %copy-start.1 = (bf16[4,8,8,64]{3,2,1,0:T(8,128)(2,1)S(1)}, bf16[4,8,8,64]{3,2,1,0:T(8,128)(2,1)}, u32[]{:S(2)}) copy-start(bf16[4,8,8,64]{3,2,1,0:T(8,128)(2,1)} %own_ref.1) | copy-start | bytes 98308
  1.0 5.3 %collective-permute-start = (bf16[1,6,2,8,128]{4,3,2,1,0:T(8,128)(2,1)S(1)}, bf16[1,6,2,8,128]{4,3,2,1,0:T(8,128)(2,1)S(1)}, u32[]{:S(2)}, u32[]{:S(2)}) collective-permute-start(bf16[1,6,2,8,128]{4,3,2,1,0:T(8,128)(2,1)S(1)} %get-tuple-element.21), channel_id=1, source_target_pairs={{0,4},{1,5},{2,6},{3,7},{4,0},{5,1},{6,2},{7,3},{8,12},{9,13},{10,... | collective-permute-start | bytes 73736 | tf_op jit(solution)/shard_map/ppermute | solution.py:358
  6.3 4.8 %copy-start = (bf16[3,3,3,16,384]{4,3,2,1,0:T(8,128)(2,1)S(1)}, bf16[3,3,3,16,384]{4,3,2,1,0:T(8,128)(2,1)}, u32[]{:S(2)}) copy-start(bf16[3,3,3,16,384]{4,3,2,1,0:T(8,128)(2,1)} %conv_in_ref.1) | copy-start | bytes 995332
  6.3 3.5 %collective-permute-start.1 = (bf16[2,4,2,8,128]{4,3,2,1,0:T(8,128)(2,1)S(1)}, bf16[2,4,2,8,128]{4,3,2,1,0:T(8,128)(2,1)S(1)}, u32[]{:S(2)}, u32[]{:S(2)}) collective-permute-start(bf16[2,4,2,8,128]{4,3,2,1,0:T(8,128)(2,1)S(1)} %get-tuple-element.25), channel_id=1, source_target_pairs={{0,2},{1,3},{2,0},{3,1},{4,6},{5,7},{6,4},{7,5},{8,10},{9,11},{10,... | collective-permute-start | bytes 98312 | tf_op jit(solution)/shard_map/ppermute | solution.py:358
  9.8 3.7 %collective-permute-start.2 = (bf16[4,3,2,8,128]{4,3,2,1,0:T(8,128)(2,1)S(1)}, bf16[4,3,2,8,128]{4,3,2,1,0:T(8,128)(2,1)S(1)}, u32[]{:S(2)}, u32[]{:S(2)}) collective-permute-start(bf16[4,3,2,8,128]{4,3,2,1,0:T(8,128)(2,1)S(1)} %get-tuple-element.29), channel_id=1, source_target_pairs={{0,1},{1,0},{2,3},{3,2},{4,5},{5,4},{6,7},{7,6},{8,9},{9,8},{10,11... | collective-permute-start | bytes 147464 | tf_op jit(solution)/shard_map/ppermute | solution.py:358
  11.3 5.4 %copy-start.2 = (f32[384]{0:T(512)S(1)}, f32[384]{0:T(512)}, u32[]{:S(2)}) copy-start(f32[384]{0:T(512)} %in_bias_ref.3) | copy-start | bytes 4612
  11.3 5.4 %copy-start.3 = (f32[384]{0:T(512)S(1)}, f32[384]{0:T(512)}, u32[]{:S(2)}) copy-start(f32[384]{0:T(512)} %gain_ref.3) | copy-start | bytes 4612
  11.3 7.1 %copy-start.4 = (f32[384]{0:T(512)S(1)}, f32[384]{0:T(512)}, u32[]{:S(2)}) copy-start(f32[384]{0:T(512)} %mid_bias_ref.1) | copy-start | bytes 4612
  13.5 4.9 %collective-permute-start.3 = (bf16[8,3,2,8,128]{4,3,2,1,0:T(8,128)(2,1)S(1)}, bf16[8,3,2,8,128]{4,3,2,1,0:T(8,128)(2,1)S(1)}, u32[]{:S(2)}, u32[]{:S(2)}) collective-permute-start(bf16[8,3,2,8,128]{4,3,2,1,0:T(8,128)(2,1)S(1)} %pad_maximum_fusion.own_ref), channel_id=1, source_target_pairs={{0,8},{8,16},{16,24},{24,0},{1,9},{9,17},{17,25},{25,1},{2,10},{10... | collective-permute-start | bytes 294920 | tf_op jit(solution)/shard_map/ppermute | solution.py:372

commit v7 on v6

--- a/solution.py
+++ b/solution.py
@@ -299,7 +299,9 @@
                         ]
             for f in range(frames):
                 for lane in range(mid // LANES):
-                    rounded[row, f, :, lane * LANES : (lane + 1) * LANES] = lines[f, lane].astype(BF16)
+                    rounded[row, f, :, lane * LANES : (lane + 1) * LANES] = lines[
+                        f, lane, : 2 * wide
+                    ].astype(BF16)
             copy = pltpu.make_async_copy(rounded.at[row], out_ref.at[:, row], sent.at[row])
             copy.start()
             return copy
@@ -454,7 +456,7 @@
             pltpu.VMEM((4, 2, early, wide, mid), BF16),
             pltpu.VMEM((2, 2, frames - late, wide, mid), BF16),
             [pltpu.VMEM((early, wide, mid), BF16) for _ in range(16)],
-            pltpu.VMEM((frames, mid // LANES, 2 * wide, LANES), F32),
+            pltpu.VMEM((frames, mid // LANES, 2 * wide + SUBLANES, LANES), F32),
             pltpu.VMEM((2, frames, 2 * wide, mid), BF16),
             pltpu.SemaphoreType.DMA((2,)),
         ],

time: 26.6 us -> 26.6 us (level)
  no operation moved by 1% of the time
where the time goes in v7:
time: 26.6 us; the launch traced here: 26.4 us
  Pallas kernels  16.1 us (61%)
  starting transfers between devices  9.1 us (34%)
  local copies, waits for them, and re-layouts  0.86 us (3%)
  between operations  0.3 us (1%)
    pallas_call x1, Pallas kernels, per_device(): pl.pallas_call(block_kernel, out_shape=jax.ShapeDtypeStruct((frames, 2, 2...  7.81 us
    pallas_call x3, Pallas kernels, beside(): pl.pallas_call(functools.partial(mixed_kernel, time), out_shape=pltpu.VME...  6.26 us
    ppermute x3, starting transfers between devices, exchanged(): got = lax.ppermute(send, axis, [(one, one ^ size) for one in range(count)])  5.87 us
    ppermute x1, starting transfers between devices, shifted(): lax.ppermute(value, axis, [(at, (at + 1) % count) for at in range(count)])  3.23 us
    pallas_call x1, Pallas kernels, per_device(): pl.pallas_call(front_kernel, out_shape=(pltpu.VMEM(windows_shape, BF16),...  1.68 us
    unnamed x10, local copies, waits for them, and re-layouts  0.86 us
  transfers between devices with their start and end apart: 4, of which 0 were waited for; matrix products, arithmetic and copies ran while one was open for 0% of the time, Pallas kernels for 31%

profile of v7, /device:TPU:1, one launch (start us, length us, event | category | flops | bytes accessed | tf_op | source)
XLA Modules:
  0.0 26.4 jit_solution(18401637966956186639)
XLA Ops:
  0.0 0.0 copy-start.1
  0.0 0.8 %copy-done.1 = bf16[4,8,8,64]{3,2,1,0:T(8,128)(2,1)S(1)} copy-done((bf16[4,8,8,64]{3,2,1,0:T(8,128)(2,1)S(1)}, bf16[4,8,8,64]{3,2,1,0:T(8,128)(2,1)}, u32[]{:S(2)}) %copy-start.1) | copy-done | bytes 32792
  0.8 0.1 chunks.1
  1.0 3.2 %collective-permute-start = (bf16[1,6,2,8,128]{4,3,2,1,0:T(8,128)(2,1)S(1)}, bf16[1,6,2,8,128]{4,3,2,1,0:T(8,128)(2,1)S(1)}, u32[]{:S(2)}, u32[]{:S(2)}) collective-permute-start(bf16[1,6,2,8,128]{4,3,2,1,0:T(8,128)(2,1)S(1)} %get-tuple-element.21), channel_id=1, source_target_pairs={{0,4},{1,5},{2,6},{3,7},{4,0},{5,1},{6,2},{7,3},{8,12},{9,13},{10,... | collective-permute-start | bytes 73736 | tf_op jit(solution)/shard_map/ppermute | solution.py:360
  4.2 2.1 %mixed.3.mixed_0_ref = bf16[16,384,384]{2,1,0:T(8,128)(2,1)S(1)} custom-call(bf16[3,3,3,384,384]{4,3,2,1,0:T(8,128)(2,1)} %conv_mid_ref.2), custom_call_target="tpu_custom_call" | custom-call | bytes 7372800 | tf_op jit(solution)/shard_map/mixed/pallas_call | solution.py:399
  6.2 0.0 collective-permute-done.got_ref
  6.3 0.0 copy-start
  6.3 1.4 %collective-permute-start.1 = (bf16[2,4,2,8,128]{4,3,2,1,0:T(8,128)(2,1)S(1)}, bf16[2,4,2,8,128]{4,3,2,1,0:T(8,128)(2,1)S(1)}, u32[]{:S(2)}, u32[]{:S(2)}) collective-permute-start(bf16[2,4,2,8,128]{4,3,2,1,0:T(8,128)(2,1)S(1)} %get-tuple-element.25), channel_id=1, source_target_pairs={{0,2},{1,3},{2,0},{3,1},{4,6},{5,7},{6,4},{7,5},{8,10},{9,11},{10,... | collective-permute-start | bytes 98312 | tf_op jit(solution)/shard_map/ppermute | solution.py:360
  7.7 2.1 %mixed.4.mixed_1_ref = bf16[16,384,384]{2,1,0:T(8,128)(2,1)S(1)} custom-call(bf16[3,3,3,384,384]{4,3,2,1,0:T(8,128)(2,1)} %conv_mid_ref.2), custom_call_target="tpu_custom_call" | custom-call | bytes 7372800 | tf_op jit(solution)/shard_map/mixed/pallas_call | solution.py:399
  9.7 0.0 collective-permute-done.1.got_ref
  9.8 1.3 %collective-permute-start.2 = (bf16[4,3,2,8,128]{4,3,2,1,0:T(8,128)(2,1)S(1)}, bf16[4,3,2,8,128]{4,3,2,1,0:T(8,128)(2,1)S(1)}, u32[]{:S(2)}, u32[]{:S(2)}) collective-permute-start(bf16[4,3,2,8,128]{4,3,2,1,0:T(8,128)(2,1)S(1)} %get-tuple-element.29), channel_id=1, source_target_pairs={{0,1},{1,0},{2,3},{3,2},{4,5},{5,4},{6,7},{7,6},{8,9},{9,8},{10,11... | collective-permute-start | bytes 147464 | tf_op jit(solution)/shard_map/ppermute | solution.py:360
  11.1 0.0 copy-done
  11.1 0.2 token_weight.1.token_weight_ref
  11.3 0.0 copy-start.2
  11.3 0.0 copy-start.3
  11.3 0.0 copy-start.4
  11.3 2.1 %mixed.5.mixed_2_ref = bf16[16,384,384]{2,1,0:T(8,128)(2,1)S(1)} custom-call(bf16[3,3,3,384,384]{4,3,2,1,0:T(8,128)(2,1)} %conv_mid_ref.2), custom_call_target="tpu_custom_call" | custom-call | bytes 7372800 | tf_op jit(solution)/shard_map/mixed/pallas_call | solution.py:399
  13.4 0.0 collective-permute-done.2
  13.5 3.2 %collective-permute-start.3 = (bf16[8,3,2,8,128]{4,3,2,1,0:T(8,128)(2,1)S(1)}, bf16[8,3,2,8,128]{4,3,2,1,0:T(8,128)(2,1)S(1)}, u32[]{:S(2)}, u32[]{:S(2)}) collective-permute-start(bf16[8,3,2,8,128]{4,3,2,1,0:T(8,128)(2,1)S(1)} %pad_maximum_fusion.own_ref), channel_id=1, source_target_pairs={{0,8},{8,16},{16,24},{24,0},{1,9},{9,17},{17,25},{25,1},{2,10},{10... | collective-permute-start | bytes 294920 | tf_op jit(solution)/shard_map/ppermute | solution.py:374
  16.7 0.0 copy-done.2
  16.7 0.0 copy-done.3
  16.7 1.7 %front.1 = (bf16[2,2,4,64,256]{4,3,2,1,0:T(8,128)(2,1)S(1)}, bf16[2,2,2,64,384]{4,3,2,1,0:T(8,128)(2,1)S(1)}, bf16[16,2,64,384]{3,2,1,0:T(8,128)(2,1)S(1)}) custom-call(bf16[8,3,2,8,128]{4,3,2,1,0:T(8,128)(2,1)S(1)} %pad_maximum_fusion.own_ref, bf16[2,3,256,768]{3,2,1,0:T(8,128)(2,1)S(1)} %token_weight.1.token_weight_ref, f32[384]{0:T(512)S(1)} %copy-done.2, ...), custom_call_target="tpu_custom_call" | custom-call | bytes 7372800 | tf_op jit(solution)/shard_map/front/pallas_call | solution.py:435
  18.4 0.0 collective-permute-done.3.previous_ref
  18.4 0.0 copy-done.4
  18.4 7.8 %block.1 = bf16[4,2,128,384]{3,2,1,0:T(8,128)(2,1)} custom-call(bf16[8,3,2,8,128]{4,3,2,1,0:T(8,128)(2,1)S(1)} %collective-permute-done.3.previous_ref, bf16[2,2,4,64,256]{4,3,2,1,0:T(8,128)(2,1)S(1)} %get-tuple-element.32.windows_ref, bf16[2,2,2,64,384]{4,3,2,1,0:T(8,128)(2,1)S(1)} %get-tuple-element.33.late_feature_ref, ...), custom_call_target="tpu_custom_call" | custom-call | tf_op jit(solution)/shard_map/block/pallas_call | solution.py:450
  (3 shorter events, 0.1 us)
Async XLA Ops:
  0.0 0.8 %copy-start.1 = (bf16[4,8,8,64]{3,2,1,0:T(8,128)(2,1)S(1)}, bf16[4,8,8,64]{3,2,1,0:T(8,128)(2,1)}, u32[]{:S(2)}) copy-start(bf16[4,8,8,64]{3,2,1,0:T(8,128)(2,1)} %own_ref.1) | copy-start | bytes 98308
  1.0 5.3 %collective-permute-start = (bf16[1,6,2,8,128]{4,3,2,1,0:T(8,128)(2,1)S(1)}, bf16[1,6,2,8,128]{4,3,2,1,0:T(8,128)(2,1)S(1)}, u32[]{:S(2)}, u32[]{:S(2)}) collective-permute-start(bf16[1,6,2,8,128]{4,3,2,1,0:T(8,128)(2,1)S(1)} %get-tuple-element.21), channel_id=1, source_target_pairs={{0,4},{1,5},{2,6},{3,7},{4,0},{5,1},{6,2},{7,3},{8,12},{9,13},{10,... | collective-permute-start | bytes 73736 | tf_op jit(solution)/shard_map/ppermute | solution.py:360
  6.3 4.8 %copy-start = (bf16[3,3,3,16,384]{4,3,2,1,0:T(8,128)(2,1)S(1)}, bf16[3,3,3,16,384]{4,3,2,1,0:T(8,128)(2,1)}, u32[]{:S(2)}) copy-start(bf16[3,3,3,16,384]{4,3,2,1,0:T(8,128)(2,1)} %conv_in_ref.1) | copy-start | bytes 995332
  6.3 3.5 %collective-permute-start.1 = (bf16[2,4,2,8,128]{4,3,2,1,0:T(8,128)(2,1)S(1)}, bf16[2,4,2,8,128]{4,3,2,1,0:T(8,128)(2,1)S(1)}, u32[]{:S(2)}, u32[]{:S(2)}) collective-permute-start(bf16[2,4,2,8,128]{4,3,2,1,0:T(8,128)(2,1)S(1)} %get-tuple-element.25), channel_id=1, source_target_pairs={{0,2},{1,3},{2,0},{3,1},{4,6},{5,7},{6,4},{7,5},{8,10},{9,11},{10,... | collective-permute-start | bytes 98312 | tf_op jit(solution)/shard_map/ppermute | solution.py:360
  9.8 3.7 %collective-permute-start.2 = (bf16[4,3,2,8,128]{4,3,2,1,0:T(8,128)(2,1)S(1)}, bf16[4,3,2,8,128]{4,3,2,1,0:T(8,128)(2,1)S(1)}, u32[]{:S(2)}, u32[]{:S(2)}) collective-permute-start(bf16[4,3,2,8,128]{4,3,2,1,0:T(8,128)(2,1)S(1)} %get-tuple-element.29), channel_id=1, source_target_pairs={{0,1},{1,0},{2,3},{3,2},{4,5},{5,4},{6,7},{7,6},{8,9},{9,8},{10,11... | collective-permute-start | bytes 147464 | tf_op jit(solution)/shard_map/ppermute | solution.py:360
  11.3 5.4 %copy-start.2 = (f32[384]{0:T(512)S(1)}, f32[384]{0:T(512)}, u32[]{:S(2)}) copy-start(f32[384]{0:T(512)} %in_bias_ref.3) | copy-start | bytes 4612
  11.3 5.4 %copy-start.3 = (f32[384]{0:T(512)S(1)}, f32[384]{0:T(512)}, u32[]{:S(2)}) copy-start(f32[384]{0:T(512)} %gain_ref.3) | copy-start | bytes 4612
  11.3 7.1 %copy-start.4 = (f32[384]{0:T(512)S(1)}, f32[384]{0:T(512)}, u32[]{:S(2)}) copy-start(f32[384]{0:T(512)} %mid_bias_ref.1) | copy-start | bytes 4612
  13.5 4.9 %collective-permute-start.3 = (bf16[8,3,2,8,128]{4,3,2,1,0:T(8,128)(2,1)S(1)}, bf16[8,3,2,8,128]{4,3,2,1,0:T(8,128)(2,1)S(1)}, u32[]{:S(2)}, u32[]{:S(2)}) collective-permute-start(bf16[8,3,2,8,128]{4,3,2,1,0:T(8,128)(2,1)S(1)} %pad_maximum_fusion.own_ref), channel_id=1, source_target_pairs={{0,8},{8,16},{16,24},{24,0},{1,9},{9,17},{17,25},{25,1},{2,10},{10... | collective-permute-start | bytes 294920 | tf_op jit(solution)/shard_map/ppermute | solution.py:374

commit v8 on v7

--- a/solution.py
+++ b/solution.py
@@ -43,10 +43,17 @@
     return sum((relative >> bit & 1) << (bits - 1 - bit) for bit in range(bits))
 
 
-def chunks_kernel(own_ref, keep_ref, send_ref):
+def chunks_kernel(tokens_ref, keep_ref, send_ref, own_ref, arrived):
     frames, rows, _, _ = own_ref.shape
+    copies = [
+        pltpu.make_async_copy(tokens_ref.at[f], own_ref.at[f], arrived.at[f]) for f in range(frames)
+    ]
+    for copy in copies:
+        copy.start()
     half = rows // 2
     mine = position() // half
+    for copy in copies:
+        copy.wait()
     for out_ref, part in ((keep_ref, mine), (send_ref, 1 - mine)):
         for at in range(half + 2):
             row = part * half + at - 1
@@ -385,9 +392,17 @@
     line = (frames // 2, cols, 2 * width)
 
     half = jax.ShapeDtypeStruct((1, tiles // 2 + 2) + line, BF16)
-    keep, send = pl.pallas_call(chunks_kernel, out_shape=(half, half), compiler_params=limited(2), name="chunks")(
-        latent_tokens
-    )
+    keep, send = pl.pallas_call(
+        chunks_kernel,
+        out_shape=(half, half),
+        in_specs=[pl.BlockSpec(memory_space=pltpu.HBM)],
+        scratch_shapes=[
+            pltpu.VMEM(latent_tokens.shape, BF16),
+            pltpu.SemaphoreType.DMA((frames,)),
+        ],
+        compiler_params=limited(2),
+        name="chunks",
+    )(far(latent_tokens))
     mixed = []
 
     def beside(value):

time: 26.6 us -> 26.7 us (level)
  local copies, waits for them, and re-layouts: 0.86 us -> 0.03 us
  Pallas kernels: 16.1 us -> 16.9 us
    unnamed x10 -> x8, local copies, waits for them, and re-layouts: 0.86 us -> 0.03 us
    pallas_call x1, Pallas kernels: 0.11 us -> 0.91 us  [per_device(): pl.pallas_call(chunks_kernel, out_shape=(half, half), in_specs=[pl.BlockS...]
where the time goes in v8:
time: 26.7 us; the launch traced here: 26.4 us
  Pallas kernels  16.9 us (63%)
  starting transfers between devices  9.1 us (34%)
  between operations  0.3 us (1%)
    pallas_call x1, Pallas kernels, per_device(): pl.pallas_call(block_kernel, out_shape=jax.ShapeDtypeStruct((frames, 2, 2...  7.81 us
    pallas_call x3, Pallas kernels, beside(): pl.pallas_call(functools.partial(mixed_kernel, time), out_shape=pltpu.VME...  6.26 us
    ppermute x3, starting transfers between devices, exchanged(): got = lax.ppermute(send, axis, [(one, one ^ size) for one in range(count)])  5.87 us
    ppermute x1, starting transfers between devices, shifted(): lax.ppermute(value, axis, [(at, (at + 1) % count) for at in range(count)])  3.23 us
    pallas_call x1, Pallas kernels, per_device(): pl.pallas_call(front_kernel, out_shape=(pltpu.VMEM(windows_shape, BF16),...  1.68 us
    pallas_call x1, Pallas kernels, per_device(): pl.pallas_call(chunks_kernel, out_shape=(half, half), in_specs=[pl.BlockS...  0.91 us
  transfers between devices with their start and end apart: 4, of which 0 were waited for; matrix products, arithmetic and copies ran while one was open for 0% of the time, Pallas kernels for 31%

profile of v8, /device:TPU:1, one launch (start us, length us, event | category | flops | bytes accessed | tf_op | source)
XLA Modules:
  0.0 26.4 jit_solution(13094560146578387834)
XLA Ops:
  0.0 0.9 %chunks.1 = (bf16[1,6,2,8,128]{4,3,2,1,0:T(8,128)(2,1)S(1)}, bf16[1,6,2,8,128]{4,3,2,1,0:T(8,128)(2,1)S(1)}) custom-call(bf16[4,8,8,64]{3,2,1,0:T(8,128)(2,1)} %tokens_ref.1), custom_call_target="tpu_custom_call" | custom-call | tf_op jit(solution)/shard_map/chunks/pallas_call | solution.py:395
  0.9 3.2 %collective-permute-start = (bf16[1,6,2,8,128]{4,3,2,1,0:T(8,128)(2,1)S(1)}, bf16[1,6,2,8,128]{4,3,2,1,0:T(8,128)(2,1)S(1)}, u32[]{:S(2)}, u32[]{:S(2)}) collective-permute-start(bf16[1,6,2,8,128]{4,3,2,1,0:T(8,128)(2,1)S(1)} %get-tuple-element.21), channel_id=1, source_target_pairs={{0,4},{1,5},{2,6},{3,7},{4,0},{5,1},{6,2},{7,3},{8,12},{9,13},{10,... | collective-permute-start | bytes 73736 | tf_op jit(solution)/shard_map/ppermute | solution.py:367
  4.1 2.1 %mixed.3.mixed_0_ref = bf16[16,384,384]{2,1,0:T(8,128)(2,1)S(1)} custom-call(bf16[3,3,3,384,384]{4,3,2,1,0:T(8,128)(2,1)} %conv_mid_ref.2), custom_call_target="tpu_custom_call" | custom-call | bytes 7372800 | tf_op jit(solution)/shard_map/mixed/pallas_call | solution.py:414
  6.2 0.0 collective-permute-done.got_ref
  6.3 0.0 copy-start
  6.3 1.4 %collective-permute-start.1 = (bf16[2,4,2,8,128]{4,3,2,1,0:T(8,128)(2,1)S(1)}, bf16[2,4,2,8,128]{4,3,2,1,0:T(8,128)(2,1)S(1)}, u32[]{:S(2)}, u32[]{:S(2)}) collective-permute-start(bf16[2,4,2,8,128]{4,3,2,1,0:T(8,128)(2,1)S(1)} %get-tuple-element.25), channel_id=1, source_target_pairs={{0,2},{1,3},{2,0},{3,1},{4,6},{5,7},{6,4},{7,5},{8,10},{9,11},{10,... | collective-permute-start | bytes 98312 | tf_op jit(solution)/shard_map/ppermute | solution.py:367
  7.6 2.1 %mixed.4.mixed_1_ref = bf16[16,384,384]{2,1,0:T(8,128)(2,1)S(1)} custom-call(bf16[3,3,3,384,384]{4,3,2,1,0:T(8,128)(2,1)} %conv_mid_ref.2), custom_call_target="tpu_custom_call" | custom-call | bytes 7372800 | tf_op jit(solution)/shard_map/mixed/pallas_call | solution.py:414
  9.7 0.0 collective-permute-done.1.got_ref
  9.8 1.3 %collective-permute-start.2 = (bf16[4,3,2,8,128]{4,3,2,1,0:T(8,128)(2,1)S(1)}, bf16[4,3,2,8,128]{4,3,2,1,0:T(8,128)(2,1)S(1)}, u32[]{:S(2)}, u32[]{:S(2)}) collective-permute-start(bf16[4,3,2,8,128]{4,3,2,1,0:T(8,128)(2,1)S(1)} %get-tuple-element.29), channel_id=1, source_target_pairs={{0,1},{1,0},{2,3},{3,2},{4,5},{5,4},{6,7},{7,6},{8,9},{9,8},{10,11... | collective-permute-start | bytes 147464 | tf_op jit(solution)/shard_map/ppermute | solution.py:367
  11.1 0.0 copy-done
  11.1 0.2 token_weight.1.token_weight_ref
  11.3 0.0 copy-start.1
  11.3 0.0 copy-start.2
  11.3 0.0 copy-start.3
  11.3 2.1 %mixed.5.mixed_2_ref = bf16[16,384,384]{2,1,0:T(8,128)(2,1)S(1)} custom-call(bf16[3,3,3,384,384]{4,3,2,1,0:T(8,128)(2,1)} %conv_mid_ref.2), custom_call_target="tpu_custom_call" | custom-call | bytes 7372800 | tf_op jit(solution)/shard_map/mixed/pallas_call | solution.py:414
  13.4 0.0 collective-permute-done.2
  13.4 3.2 %collective-permute-start.3 = (bf16[8,3,2,8,128]{4,3,2,1,0:T(8,128)(2,1)S(1)}, bf16[8,3,2,8,128]{4,3,2,1,0:T(8,128)(2,1)S(1)}, u32[]{:S(2)}, u32[]{:S(2)}) collective-permute-start(bf16[8,3,2,8,128]{4,3,2,1,0:T(8,128)(2,1)S(1)} %pad_maximum_fusion.own_ref), channel_id=1, source_target_pairs={{0,8},{8,16},{16,24},{24,0},{1,9},{9,17},{17,25},{25,1},{2,10},{10... | collective-permute-start | bytes 294920 | tf_op jit(solution)/shard_map/ppermute | solution.py:381
  16.7 0.0 copy-done.1
  16.7 0.0 copy-done.2
  16.7 1.7 %front.1 = (bf16[2,2,4,64,256]{4,3,2,1,0:T(8,128)(2,1)S(1)}, bf16[2,2,2,64,384]{4,3,2,1,0:T(8,128)(2,1)S(1)}, bf16[16,2,64,384]{3,2,1,0:T(8,128)(2,1)S(1)}) custom-call(bf16[8,3,2,8,128]{4,3,2,1,0:T(8,128)(2,1)S(1)} %pad_maximum_fusion.own_ref, bf16[2,3,256,768]{3,2,1,0:T(8,128)(2,1)S(1)} %token_weight.1.token_weight_ref, f32[384]{0:T(512)S(1)} %copy-done.1, ...), custom_call_target="tpu_custom_call" | custom-call | bytes 7372800 | tf_op jit(solution)/shard_map/front/pallas_call | solution.py:450
  18.4 0.0 collective-permute-done.3.previous_ref
  18.4 0.0 copy-done.3
  18.4 7.8 %block.1 = bf16[4,2,128,384]{3,2,1,0:T(8,128)(2,1)} custom-call(bf16[8,3,2,8,128]{4,3,2,1,0:T(8,128)(2,1)S(1)} %collective-permute-done.3.previous_ref, bf16[2,2,4,64,256]{4,3,2,1,0:T(8,128)(2,1)S(1)} %get-tuple-element.32.windows_ref, bf16[2,2,2,64,384]{4,3,2,1,0:T(8,128)(2,1)S(1)} %get-tuple-element.33.late_feature_ref, ...), custom_call_target="tpu_custom_call" | custom-call | tf_op jit(solution)/shard_map/block/pallas_call | solution.py:465
  (3 shorter events, 0.1 us)
Async XLA Ops:
  0.9 5.3 %collective-permute-start = (bf16[1,6,2,8,128]{4,3,2,1,0:T(8,128)(2,1)S(1)}, bf16[1,6,2,8,128]{4,3,2,1,0:T(8,128)(2,1)S(1)}, u32[]{:S(2)}, u32[]{:S(2)}) collective-permute-start(bf16[1,6,2,8,128]{4,3,2,1,0:T(8,128)(2,1)S(1)} %get-tuple-element.21), channel_id=1, source_target_pairs={{0,4},{1,5},{2,6},{3,7},{4,0},{5,1},{6,2},{7,3},{8,12},{9,13},{10,... | collective-permute-start | bytes 73736 | tf_op jit(solution)/shard_map/ppermute | solution.py:367
  6.3 4.8 %copy-start = (bf16[3,3,3,16,384]{4,3,2,1,0:T(8,128)(2,1)S(1)}, bf16[3,3,3,16,384]{4,3,2,1,0:T(8,128)(2,1)}, u32[]{:S(2)}) copy-start(bf16[3,3,3,16,384]{4,3,2,1,0:T(8,128)(2,1)} %conv_in_ref.1) | copy-start | bytes 995332
  6.3 3.5 %collective-permute-start.1 = (bf16[2,4,2,8,128]{4,3,2,1,0:T(8,128)(2,1)S(1)}, bf16[2,4,2,8,128]{4,3,2,1,0:T(8,128)(2,1)S(1)}, u32[]{:S(2)}, u32[]{:S(2)}) collective-permute-start(bf16[2,4,2,8,128]{4,3,2,1,0:T(8,128)(2,1)S(1)} %get-tuple-element.25), channel_id=1, source_target_pairs={{0,2},{1,3},{2,0},{3,1},{4,6},{5,7},{6,4},{7,5},{8,10},{9,11},{10,... | collective-permute-start | bytes 98312 | tf_op jit(solution)/shard_map/ppermute | solution.py:367
  9.8 3.7 %collective-permute-start.2 = (bf16[4,3,2,8,128]{4,3,2,1,0:T(8,128)(2,1)S(1)}, bf16[4,3,2,8,128]{4,3,2,1,0:T(8,128)(2,1)S(1)}, u32[]{:S(2)}, u32[]{:S(2)}) collective-permute-start(bf16[4,3,2,8,128]{4,3,2,1,0:T(8,128)(2,1)S(1)} %get-tuple-element.29), channel_id=1, source_target_pairs={{0,1},{1,0},{2,3},{3,2},{4,5},{5,4},{6,7},{7,6},{8,9},{9,8},{10,11... | collective-permute-start | bytes 147464 | tf_op jit(solution)/shard_map/ppermute | solution.py:367
  11.3 5.4 %copy-start.1 = (f32[384]{0:T(512)S(1)}, f32[384]{0:T(512)}, u32[]{:S(2)}) copy-start(f32[384]{0:T(512)} %in_bias_ref.3) | copy-start | bytes 4612
  11.3 5.4 %copy-start.2 = (f32[384]{0:T(512)S(1)}, f32[384]{0:T(512)}, u32[]{:S(2)}) copy-start(f32[384]{0:T(512)} %gain_ref.3) | copy-start | bytes 4612
  11.3 7.1 %copy-start.3 = (f32[384]{0:T(512)S(1)}, f32[384]{0:T(512)}, u32[]{:S(2)}) copy-start(f32[384]{0:T(512)} %mid_bias_ref.1) | copy-start | bytes 4612
  13.4 4.9 %collective-permute-start.3 = (bf16[8,3,2,8,128]{4,3,2,1,0:T(8,128)(2,1)S(1)}, bf16[8,3,2,8,128]{4,3,2,1,0:T(8,128)(2,1)S(1)}, u32[]{:S(2)}, u32[]{:S(2)}) collective-permute-start(bf16[8,3,2,8,128]{4,3,2,1,0:T(8,128)(2,1)S(1)} %pad_maximum_fusion.own_ref), channel_id=1, source_target_pairs={{0,8},{8,16},{16,24},{24,0},{1,9},{9,17},{17,25},{25,1},{2,10},{10... | collective-permute-start | bytes 294920 | tf_op jit(solution)/shard_map/ppermute | solution.py:381
